TPU v7x, 32 devices: a whole 2x2x4 slice. The times are simulated.
32 devices in a mesh: rows: 8 (over z, y), samples: 4 (over x, core).
Axes of the slice: x: 2, y: 2, z: 4, core: 2. Of those that a mesh axis runs over, the one named last changes fastest.
Arguments:
- matrix_block: bfloat16 [8192, 10240], P('rows', 'samples'), may hold values from -6 to 6
- sketch_matrix: bfloat16 [10240, 384], P('samples'), may hold values from -0.0625 to 0.0625
- local_pivots: int32 [8, 3, 256], P('rows'), may hold values from 0 to 511, as said below
- upper_pivots: int32 [6, 256], replicated, may hold values from 0 to 511, as said below
Outputs:
- leaf_basis: float32 [8192, 384], P(('rows', 'samples'))
- device_basis: float32 [4096, 384], P('rows')
- inner_basis: float32 [4096, 384], P('rows')
Inputs may be any that keep to these rules, and one draw needn't show every extreme that they name: `local_pivots`: each row holds 256 distinct indices. `upper_pivots`: each row holds 256 distinct indices.
All inputs are finite; a program needn't handle non-finite values.
Results may differ from a plain program's by a relative error of at most 0.0003.
Values sent between devices are 32-bit elements; how exact they have to be, the bound alone decides.
No kernel may reach another device: no remote copies, remote signals or barrier semaphores. Data moves between devices by JAX's collectives and lax.ppermute only.
A program may use at most 128 MiB of HBM per device.

v0:
```python
import functools
import math

import jax
import jax.numpy as jnp
from jax import lax
from jax.experimental import pallas as pl
from jax.experimental.pallas import tpu as pltpu
from jax.sharding import PartitionSpec as P

F32 = jnp.float32
BF16 = jnp.bfloat16
PANEL = 128
STRIP = 32
AHEAD = 5


def dot_of(left, right, left_dim, right_dim):
    return lax.dot_general(
        left, right, (((left_dim,), (right_dim,)), ((), ())), preferred_element_type=F32
    )


def halves(value):
    high = value.astype(BF16)
    return high, (value - high.astype(F32)).astype(BF16)


def dot3(left, right, left_dim, right_dim):
    left_high, left_low = halves(left)
    right_high, right_low = halves(right)
    cross = dot_of(left_high, right_low, left_dim, right_dim)
    cross += dot_of(left_low, right_high, left_dim, right_dim)
    return dot_of(left_high, right_high, left_dim, right_dim) + cross


def spread_row(tile, row):
    return jnp.broadcast_to(tile[row : row + 1], tile.shape)


def spread_lane(tile, lane):
    return jnp.broadcast_to(tile[:, lane : lane + 1], tile.shape)


def eliminate(strips, first, width):
    tiles = STRIP // 8
    lane = lax.broadcasted_iota(jnp.int32, (8, width), 1)
    sub = lax.broadcasted_iota(jnp.int32, (8, width), 0)
    rows = [[strip[8 * t : 8 * t + 8] for t in range(tiles)] for strip in strips]
    pivots = [[None] * tiles for _ in strips]
    columns = [
        {k: {t: spread_lane(own[t], first + k) for t in range(tiles)} for k in range(AHEAD + 1)}
        for own in rows
    ]
    for j in range(STRIP):
        at, row = j // 8, j % 8
        below = sub > row
        here = lane == first + j
        for own, ahead, seen in zip(rows, columns, pivots):
            column = ahead.pop(j)
            pivot = spread_row(column[at], row)
            seen[at] = pivot if row == 0 else jnp.where(sub >= row, pivot, seen[at])
            inverse = pl.reciprocal(pivot, approx=True)
            factor = {t: column[t] for t in range(at + 1, tiles)}
            if row < 7:
                factor[at] = jnp.where(below, column[at], 0.0)
            for later in ahead.values():
                value = spread_row(later[at], row)
                for t in later:
                    if t in factor:
                        later[t] = later[t] - (factor[t] * value) * inverse
            pivot_row = jnp.where(here, 1.0, spread_row(own[at], row)) * inverse
            for t in factor:
                cleared = jnp.logical_and(here, below) if t == at else here
                own[t] = jnp.where(cleared, 0.0, own[t]) - factor[t] * pivot_row
            new = j + AHEAD + 1
            if new < STRIP:
                ahead[new] = {
                    t: spread_lane(own[t], first + new) for t in range((j + 1) // 8, tiles)
                }
    scaled = []
    for own, seen in zip(rows, pivots):
        out = []
        for t in range(tiles):
            offset = lane - first - 8 * t
            tile = jnp.where(offset == sub, 1.0, own[t])
            tile = jnp.where(jnp.logical_and(offset > sub, lane < first + STRIP), 0.0, tile)
            out.append(tile * lax.rsqrt(seen[t]))
        scaled.append(jnp.concatenate(out, 0))
    return scaled


def panel_inverses(panels):
    width = panels[0].shape[0]
    rest = list(panels)
    inverse_rows = [[] for _ in panels]
    for first in range(0, width, STRIP):
        past = first + STRIP
        strips = eliminate([one[:STRIP] for one in rest], first, width)
        lane = lax.broadcasted_iota(jnp.int32, (STRIP, width), 1)
        for m, strip in enumerate(strips):
            inverse_rows[m].append(jnp.where(lane < past, strip, 0.0))
            if past < width:
                update = dot3(strip, strip, 0, 0)[past:]
                below = rest[m][STRIP:]
                lanes = lax.broadcasted_iota(jnp.int32, below.shape, 1)
                done = jnp.logical_and(lanes >= first, lanes < past)
                rest[m] = jnp.where(done, 0.0, below) - update
    return [jnp.concatenate(parts, 0) for parts in inverse_rows]


def basis_kernel(*refs, count):
    stacked, bases = refs[:count], refs[count : 2 * count]
    grams, left = refs[2 * count : 3 * count], refs[3 * count :]
    rows, columns = stacked[0].shape
    scale = math.sqrt(rows)
    for source, gram in zip(stacked, grams):
        value = source[...]
        gram[...] = dot3(value, value, 0, 0)
    for start in range(0, columns, PANEL):
        own, after = slice(start, start + PANEL), slice(start + PANEL, columns)
        last = start + PANEL == columns
        inverses = panel_inverses([gram[own, own] for gram in grams])
        for inverse, source, gram, basis, rest in zip(inverses, stacked, grams, bases, left):
            held = source if start == 0 else rest
            if not last:
                lower = dot3(gram[after, own], inverse, 1, 1)
                gram[after, after] = gram[after, after] - dot3(lower, lower, 1, 1)
            block = dot3(held[:, own], inverse, 1, 1)
            basis[:, own] = block * scale
            if not last:
                rest[:, after] = held[:, after] - dot3(block, lower, 1, 1)


def bases_of(stacked):
    count = len(stacked)
    rows, columns = stacked[0].shape
    vmem = pl.BlockSpec(memory_space=pltpu.VMEM)
    shape = jax.ShapeDtypeStruct((rows, columns), F32)
    return pl.pallas_call(
        functools.partial(basis_kernel, count=count),
        out_shape=[shape] * count,
        in_specs=[vmem] * count,
        out_specs=[vmem] * count,
        scratch_shapes=[pltpu.VMEM((columns, columns), F32)] * count
        + [pltpu.VMEM((rows, columns), F32)] * count,
        compiler_params=pltpu.CompilerParams(vmem_limit_bytes=48 << 20),
        name="bases",
    )(*stacked)


def partner_2(block, axis, bit):
    count = lax.axis_size(axis)
    route = []
    for low in range(count):
        high = low | 1 << bit
        if high != low and high < count:
            route += [(low, high), (high, low)]
    return lax.ppermute(block, axis, route)


def select_rows(matrix_rows, indices):
    return jnp.take(matrix_rows, indices, axis=0)


def climb_tree(current, tree_depth, position, upper_pivots):
    chosen = None
    for height in range(1, tree_depth + 1):
        partner = partner_2(current, "rows", height - 1)
        on_right = position >> height - 1 & 1 == 1
        left_part = jnp.where(on_right, partner, current)
        right_part = jnp.where(on_right, current, partner)
        stacked = jnp.concatenate([left_part, right_part], 0)
        low_bits = position & (1 << height) - 1
        is_owner = low_bits == 1 << height - 1
        if height == tree_depth:
            is_owner = jnp.logical_or(is_owner, position == 0)
        chosen = stacked if chosen is None else jnp.where(is_owner, stacked, chosen)
        if height < tree_depth:
            node_row = (1 << tree_depth - height) + (position >> height) - 2
            indices = lax.dynamic_index_in_dim(upper_pivots, node_row, 0, keepdims=False)
            current = select_rows(stacked, indices)
    return chosen


def on_device(matrix_block, sketch_matrix, local_pivots, upper_pivots):
    leaf_rows = matrix_block.shape[0] // 2
    partial_value = jnp.dot(matrix_block, sketch_matrix, preferred_element_type=jnp.float32)
    pivots = local_pivots[0]
    summed = lax.psum(partial_value, "samples")
    first_leaf = summed[:leaf_rows]
    second_leaf = summed[leaf_rows:]
    skeleton_a = select_rows(first_leaf, pivots[0])
    skeleton_b = select_rows(second_leaf, pivots[1])
    stacked = jnp.concatenate([skeleton_a, skeleton_b], 0)
    current = select_rows(stacked, pivots[2])
    tree_depth = lax.axis_size("rows").bit_length() - 1
    position = lax.axis_index("rows")
    node = climb_tree(current, tree_depth, position, upper_pivots)

    share = lax.axis_index("samples")
    shares = lax.axis_size("samples")
    second_half = share >= shares // 2
    own_leaf = jnp.where(second_half, second_leaf, first_leaf)
    leaf_basis, device_out, node_out = bases_of([own_leaf, stacked, node])
    share_rows = 2 * leaf_rows // shares
    leaf_out = lax.dynamic_slice_in_dim(
        leaf_basis, share % (shares // 2) * share_rows, share_rows, 0
    )
    return (leaf_out, device_out, node_out)


def solution(mesh):
    in_specs = (P("rows", "samples"), P("samples", None), P("rows", None, None), P())
    out_specs = (P(("rows", "samples"), None), P("rows", None), P("rows", None))
    return jax.shard_map(
        on_device, mesh=mesh, in_specs=in_specs, out_specs=out_specs, check_vma=False
    )
```

profile of v0, /device:TPU:0, one launch (start us, length us, event | category | flops | bytes accessed | tf_op | source)
XLA Modules:
  0.0 165.0 jit_solution(72504292559582876)
XLA Ops:
  7.2 0.0 copy-start
  7.2 0.0 copy-start.7
  7.2 0.0 all-reduce.2.cloned.1.call-start
  7.2 1.5 copy-done
  8.7 6.5 %fusion.2 = f32[1024,384]{1,0:T(8,128)} fusion(bf16[1024,2560]{1,0:T(8,128)(2,1)} %param.6, bf16[2560,384]{1,0:T(8,128)(2,1)S(1)} %copy-done), kind=kOutput, calls=%fused_computation.41 | convolution fusion | flops 2013265920 | bytes 8781824 | tf_op jit(solution)/shard_map/dot_general | solution.py:188
  15.2 0.0 all-reduce.2.cloned.1.call-update
  15.2 0.0 copy-done.7
  15.3 0.8 constant_dynamic-slice_fusion.1
  16.1 0.6 pad_clamp_fusion.4
  16.7 0.5 compare_and_fusion.4
  17.2 0.6 compare_and_fusion.2
  17.8 43.1 %all-reduce.2.cloned.1.call-done = f32[1024,384]{1,0:T(8,128)} async-done(((f32[1024,384]{1,0:T(8,128)}), f32[1024,384]{1,0:T(8,128)}) %all-reduce.2.cloned.1.call-update) | async-done | bytes 1572880 | tf_op jit(solution)/shard_map/psum | solution.py:190
  60.9 2.4 %fusion = (f32[512,384]{1,0:T(8,128)}, f32[512,384]{1,0:T(8,128)S(1)}, f32[512,384]{1,0:T(8,128)S(1)}) fusion(f32[1024,384]{1,0:T(8,128)} %all-reduce.2.cloned.1.call-done, pred[]{:T(512)S(6)} %ge.8), kind=kLoop, calls=%fused_computation.39 | loop fusion | flops 196608 | bytes 3932161 | tf_op jit(solution)/shard_map/slice | solution.py:191
  63.3 3.1 %gather_fusion = f32[256,384]{1,0:T(8,128)} fusion(f32[512,384]{1,0:T(8,128)} %get-tuple-element.10, s32[1024]{0:T(1024)} %pad_clamp_fusion.4), kind=kCustom, calls=%fused_computation.clone | custom fusion | bytes 787456 | tf_op jit(solution)/shard_map/jit(_take)/gather | solution.py:163
  66.5 1.8 %broadcast_select_fusion.5 = f32[256,384]{1,0:T(8,128)} fusion(f32[256,384]{1,0:T(8,128)} %gather_fusion, pred[256]{0:T(512)(128)(4,1)} %compare_and_fusion.4), kind=kLoop, calls=%fused_computation.14 | loop fusion | flops 98304 | bytes 786688 | tf_op jit(solution)/shard_map/jit(_take)/select_n | solution.py:163
  68.3 1.7 %gather_fusion.1 = f32[256,384]{1,0:T(8,128)} fusion(f32[512,384]{1,0:T(8,128)S(1)} %get-tuple-element.12, s32[1024]{0:T(1024)S(1)} %pad_clamp_fusion.3), kind=kCustom, calls=%fused_computation.1.clone | custom fusion | bytes 787456 | tf_op jit(solution)/shard_map/jit(_take)/gather | solution.py:163
  70.0 1.1 broadcast_select_fusion.4
  71.1 1.1 pad_maximum_fusion.refs_1_
  72.2 0.0 copy-start.5
  72.2 1.7 %gather_fusion.2 = f32[256,384]{1,0:T(8,128)} fusion(f32[512,384]{1,0:T(8,128)S(1)} %pad_maximum_fusion.refs_1_, s32[1024]{0:T(1024)S(1)} %pad_clamp_fusion.2), kind=kCustom, calls=%fused_computation.2.clone | custom fusion | bytes 787456 | tf_op jit(solution)/shard_map/jit(_take)/gather | solution.py:163
  73.9 0.0 copy-done.5
  73.9 1.8 %broadcast_select_fusion.3 = f32[256,384]{1,0:T(8,128)} fusion(f32[256,384]{1,0:T(8,128)} %gather_fusion.2, pred[256]{0:T(512)(128)(4,1)S(1)} %copy-done.5), kind=kLoop, calls=%fused_computation.12 | loop fusion | flops 98304 | bytes 786688 | tf_op jit(solution)/shard_map/jit(_take)/select_n | solution.py:163
  75.8 1.5 collective-permute-start
  77.3 0.5 compare_and_fusion
  77.8 9.0 %collective-permute-done = f32[256,384]{1,0:T(8,128)} collective-permute-done((f32[256,384]{1,0:T(8,128)}, f32[256,384]{1,0:T(8,128)}, u32[]{:S(2)}, u32[]{:S(2)}) %collective-permute-start) | collective-permute-done | bytes 393248 | tf_op jit(solution)/shard_map/ppermute | solution.py:159
  86.8 1.2 broadcast_select_fusion.7
  88.0 0.0 copy-start.1
  88.1 0.0 copy-start.2
  88.1 0.7 copy-done.1
  88.8 0.1 copy-done.2
  88.9 0.9 pad_maximum_fusion.1
  89.9 3.0 %gather_fusion.3 = f32[256,384]{1,0:T(8,128)} fusion(f32[512,384]{1,0:T(8,128)} %pad_maximum_fusion.1, s32[1024]{0:T(1024)S(1)} %pad_clamp_fusion.1), kind=kCustom, calls=%fused_computation.3.clone | custom fusion | bytes 787456 | tf_op jit(solution)/shard_map/jit(_take)/gather | solution.py:163
  92.9 1.8 %broadcast_select_fusion.2 = f32[256,384]{1,0:T(8,128)} fusion(f32[256,384]{1,0:T(8,128)} %gather_fusion.3, pred[256]{0:T(512)(128)(4,1)S(1)} %copy-done.6), kind=kLoop, calls=%fused_computation.11 | loop fusion | flops 98304 | bytes 786688 | tf_op jit(solution)/shard_map/jit(_take)/select_n | solution.py:163
  94.7 1.5 collective-permute-start.1
  96.2 8.6 %collective-permute-done.1 = f32[256,384]{1,0:T(8,128)} collective-permute-done((f32[256,384]{1,0:T(8,128)}, f32[256,384]{1,0:T(8,128)}, u32[]{:S(2)}, u32[]{:S(2)}) %collective-permute-start.1) | collective-permute-done | bytes 393248 | tf_op jit(solution)/shard_map/ppermute | solution.py:159
  104.9 1.2 broadcast_select_fusion.9
  106.1 0.0 copy-start.4
  106.1 0.7 copy-done.3
  106.9 0.1 copy-done.4
  107.0 0.9 pad_maximum_fusion.2
  107.9 3.0 %gather_fusion.4 = f32[256,384]{1,0:T(8,128)} fusion(f32[512,384]{1,0:T(8,128)} %pad_maximum_fusion.2, s32[1024]{0:T(1024)S(1)} %pad_clamp_fusion), kind=kCustom, calls=%fused_computation.4.clone | custom fusion | bytes 787456 | tf_op jit(solution)/shard_map/jit(_take)/gather | solution.py:163
  110.9 1.8 %broadcast_select_fusion.1 = f32[256,384]{1,0:T(8,128)} fusion(f32[256,384]{1,0:T(8,128)} %gather_fusion.4, pred[256]{0:T(512)(128)(4,1)S(1)} %get-tuple-element.26), kind=kLoop, calls=%fused_computation.10 | loop fusion | flops 98304 | bytes 786688 | tf_op jit(solution)/shard_map/jit(_take)/select_n | solution.py:163
  112.8 2.4 %collective-permute-start.2 = (f32[256,384]{1,0:T(8,128)}, f32[256,384]{1,0:T(8,128)}, u32[]{:S(2)}, u32[]{:S(2)}) collective-permute-start(f32[256,384]{1,0:T(8,128)} %broadcast_select_fusion.1), channel_id=1, source_target_pairs={{0,16},{16,0},{4,20},{20,4},{8,24},{24,8},{12,28},{28,12},{1,17},{... | collective-permute-start | bytes 1179656 | tf_op jit(solution)/shard_map/ppermute | solution.py:159
  115.2 16.1 %collective-permute-done.2 = f32[256,384]{1,0:T(8,128)} collective-permute-done((f32[256,384]{1,0:T(8,128)}, f32[256,384]{1,0:T(8,128)}, u32[]{:S(2)}, u32[]{:S(2)}) %collective-permute-start.2) | collective-permute-done | bytes 393248 | tf_op jit(solution)/shard_map/ppermute | solution.py:159
  131.3 1.2 broadcast_select_fusion.11
  132.5 1.5 maximum_select_fusion.refs_2_
  134.0 23.4 %bases.1 = (f32[512,384]{1,0:T(8,128)S(1)}, f32[512,384]{1,0:T(8,128)}, f32[512,384]{1,0:T(8,128)}) custom-call(f32[512,384]{1,0:T(8,128)S(1)} %get-tuple-element.11.refs_0_, f32[512,384]{1,0:T(8,128)S(1)} %pad_maximum_fusion.refs_1_, f32[512,384]{1,0:T(8,128)S(1)} %maximum_select_fusion.refs_2_), custom_call_target="tpu_custom_call" | custom-call | tf_op jit(solution)/shard_map/bases/pallas_call | solution.py:140
  157.4 0.8 constant_dynamic-slice_fusion
  (12 shorter events, 0.1 us)
Async XLA Ops:
  7.2 1.6 copy-start
  7.2 8.0 %copy-start.7 = (s32[1,3,256]{2,0,1:T(1,128)S(1)}, s32[1,3,256]{2,0,1:T(1,128)}, u32[]{:S(2)}) copy-start(s32[1,3,256]{2,0,1:T(1,128)} %param.8) | copy-start | bytes 9220
  7.2 53.7 %all-reduce.2.cloned.1.call-start = ((), (), s32[]{:S(2)}) async-start(), calls=%async_computation | async-start | bytes 3145728 | tf_op jit(solution)/shard_map/psum | solution.py:190
  72.2 1.7 %copy-start.5 = (pred[256]{0:T(512)(128)(4,1)S(1)}, pred[256]{0:T(512)(128)(4,1)}, u32[]{:S(2)}) copy-start(pred[256]{0:T(512)(128)(4,1)} %get-tuple-element.28) | copy-start | bytes 772
  75.8 11.0 %collective-permute-start = (f32[256,384]{1,0:T(8,128)}, f32[256,384]{1,0:T(8,128)}, u32[]{:S(2)}, u32[]{:S(2)}) collective-permute-start(f32[256,384]{1,0:T(8,128)} %broadcast_select_fusion.3), channel_id=1, source_target_pairs={{0,4},{4,0},{8,12},{12,8},{16,20},{20,16},{24,28},{28,24},{1,5},{5... | collective-permute-start | bytes 1179656 | tf_op jit(solution)/shard_map/ppermute | solution.py:159
  88.0 0.7 copy-start.1
  88.1 0.9 copy-start.2
  89.9 3.0 %copy-start.6 = (pred[256]{0:T(512)(128)(4,1)S(1)}, pred[256]{0:T(512)(128)(4,1)}, u32[]{:S(2)}) copy-start(pred[256]{0:T(512)(128)(4,1)} %get-tuple-element.27) | copy-start | bytes 772
  94.7 10.1 %collective-permute-start.1 = (f32[256,384]{1,0:T(8,128)}, f32[256,384]{1,0:T(8,128)}, u32[]{:S(2)}, u32[]{:S(2)}) collective-permute-start(f32[256,384]{1,0:T(8,128)} %broadcast_select_fusion.2), channel_id=1, source_target_pairs={{0,8},{8,0},{4,12},{12,4},{16,24},{24,16},{20,28},{28,20},{1,9},{9... | collective-permute-start | bytes 1179656 | tf_op jit(solution)/shard_map/ppermute | solution.py:159
  106.1 0.8 copy-start.3
  106.1 0.9 copy-start.4
  112.8 18.5 %collective-permute-start.2 = (f32[256,384]{1,0:T(8,128)}, f32[256,384]{1,0:T(8,128)}, u32[]{:S(2)}, u32[]{:S(2)}) collective-permute-start(f32[256,384]{1,0:T(8,128)} %broadcast_select_fusion.1), channel_id=1, source_target_pairs={{0,16},{16,0},{4,20},{20,4},{8,24},{24,8},{12,28},{28,12},{1,17},{... | collective-permute-start | bytes 1179656 | tf_op jit(solution)/shard_map/ppermute | solution.py:159
Sparse Core Ops, SparseCore 0:
  15.3 45.5 all-reduce.1
where the time goes:
time: 166 us; the launch traced here: 165 us
  waiting for transfers between devices  77 us (46%)
  Pallas kernels  23.4 us (14%)
  other arithmetic  21.2 us (13%)
  local copies, waits for them, and re-layouts  17.4 us (10%)
  between operations  14.2 us (9%)
  matrix products  6.47 us (4%)
  starting transfers between devices  5.4 us (3%)
    psum x1, waiting for transfers between devices, on_device(): summed = lax.psum(partial_value, 'samples')  43.1 us
    ppermute x3, waiting for transfers between devices, partner_2(): return lax.ppermute(block, axis, route)  33.8 us
    pallas_call x1, Pallas kernels, bases_of(): pl.pallas_call(functools.partial(basis_kernel, count=count), out_shape=[s...  23.4 us
    gather x5, local copies, waits for them, and re-layouts, select_rows(): return jnp.take(matrix_rows, indices, axis=0)  12.6 us
    select_n x9, other arithmetic, select_rows(): return jnp.take(matrix_rows, indices, axis=0)  8.49 us
    dot_general x1, matrix products, on_device(): jnp.dot(matrix_block, sketch_matrix, preferred_element_type=jnp.float32)  6.47 us
    ppermute x3, starting transfers between devices, partner_2(): return lax.ppermute(block, axis, route)  5.37 us
    select_n x3, other arithmetic, climb_tree(): left_part = jnp.where(on_right, partner, current)  3.7 us
  transfers between devices with their start and end apart: 4, of which 4 were waited for; matrix products, arithmetic and copies ran while one was open for 2% of the time, Pallas kernels for 0%

commit v1 on v0

v1 whole, which is shorter than its diff:
```python
import functools
import math

import jax
import jax.numpy as jnp
from jax import lax
from jax.experimental import pallas as pl
from jax.experimental.pallas import tpu as pltpu
from jax.sharding import PartitionSpec as P

F32 = jnp.float32
BF16 = jnp.bfloat16
PANEL = 128
STRIP = 32
AHEAD = 5
PRODUCT_VMEM = 61 << 20
SMALL_VMEM = 12 << 20
BASES_VMEM = 24 << 20
VMEM = pl.BlockSpec(memory_space=pltpu.VMEM)
SMEM = pl.BlockSpec(memory_space=pltpu.SMEM)


def dot_of(left, right, left_dim, right_dim):
    return lax.dot_general(
        left, right, (((left_dim,), (right_dim,)), ((), ())), preferred_element_type=F32
    )


def halves(value):
    high = value.astype(BF16)
    return high, (value - high.astype(F32)).astype(BF16)


def dot3(left, right, left_dim, right_dim):
    left_high, left_low = halves(left)
    right_high, right_low = halves(right)
    cross = dot_of(left_high, right_low, left_dim, right_dim)
    cross += dot_of(left_low, right_high, left_dim, right_dim)
    return dot_of(left_high, right_high, left_dim, right_dim) + cross


def spread_row(tile, row):
    return jnp.broadcast_to(tile[row : row + 1], tile.shape)


def spread_lane(tile, lane):
    return jnp.broadcast_to(tile[:, lane : lane + 1], tile.shape)


def eliminate(strips, first, width):
    tiles = STRIP // 8
    lane = lax.broadcasted_iota(jnp.int32, (8, width), 1)
    sub = lax.broadcasted_iota(jnp.int32, (8, width), 0)
    rows = [[strip[8 * t : 8 * t + 8] for t in range(tiles)] for strip in strips]
    pivots = [[None] * tiles for _ in strips]
    columns = [
        {k: {t: spread_lane(own[t], first + k) for t in range(tiles)} for k in range(AHEAD + 1)}
        for own in rows
    ]
    for j in range(STRIP):
        at, row = j // 8, j % 8
        below = sub > row
        here = lane == first + j
        for own, ahead, seen in zip(rows, columns, pivots):
            column = ahead.pop(j)
            pivot = spread_row(column[at], row)
            seen[at] = pivot if row == 0 else jnp.where(sub >= row, pivot, seen[at])
            inverse = pl.reciprocal(pivot, approx=True)
            factor = {t: column[t] for t in range(at + 1, tiles)}
            if row < 7:
                factor[at] = jnp.where(below, column[at], 0.0)
            for later in ahead.values():
                value = spread_row(later[at], row) * inverse
                for t in later:
                    if t in factor:
                        later[t] = later[t] - factor[t] * value
            pivot_row = jnp.where(here, 1.0, spread_row(own[at], row)) * inverse
            for t in factor:
                cleared = jnp.logical_and(here, below) if t == at else here
                own[t] = jnp.where(cleared, 0.0, own[t]) - factor[t] * pivot_row
            new = j + AHEAD + 1
            if new < STRIP:
                ahead[new] = {
                    t: spread_lane(own[t], first + new) for t in range((j + 1) // 8, tiles)
                }
    scaled = []
    for own, seen in zip(rows, pivots):
        out = []
        for t in range(tiles):
            offset = lane - first - 8 * t
            tile = jnp.where(offset == sub, 1.0, own[t])
            tile = jnp.where(jnp.logical_and(offset > sub, lane < first + STRIP), 0.0, tile)
            out.append(tile * lax.rsqrt(seen[t]))
        scaled.append(jnp.concatenate(out, 0))
    return scaled


def panel_inverses(panels):
    width = panels[0].shape[0]
    rest = list(panels)
    inverse_rows = [[] for _ in panels]
    for first in range(0, width, STRIP):
        past = first + STRIP
        strips = eliminate([one[:STRIP] for one in rest], first, width)
        lane = lax.broadcasted_iota(jnp.int32, (STRIP, width), 1)
        for m, strip in enumerate(strips):
            inverse_rows[m].append(jnp.where(lane < past, strip, 0.0))
            if past < width:
                update = dot3(strip, strip, 0, 0)[past:]
                below = rest[m][STRIP:]
                lanes = lax.broadcasted_iota(jnp.int32, below.shape, 1)
                done = jnp.logical_and(lanes >= first, lanes < past)
                rest[m] = jnp.where(done, 0.0, below) - update
    return [jnp.concatenate(parts, 0) for parts in inverse_rows]


def basis_kernel(*refs, count, bits):
    place, parts, bases = refs[0], refs[1 : 1 + 2 * count], refs[1 + 2 * count : 1 + 3 * count]
    held, grams = refs[1 + 3 * count : 1 + 4 * count], refs[1 + 4 * count : 1 + 5 * count]
    leaf = refs[1 + 5 * count]
    columns, rows = held[0].shape
    scale = math.sqrt(rows)
    half = columns // 2
    for m, source in enumerate(held):
        source[pl.ds(pl.multiple_of(place[0] * half, half), half), :] = parts[2 * m][...]
        source[pl.ds(pl.multiple_of(half - place[0] * half, half), half), :] = parts[2 * m + 1][...]
    for source, gram in zip(held, grams):
        value = source[...]
        gram[...] = dot3(value, value, 1, 1)
    share = bases[0].shape[0]
    index = sum(place[b] << b for b in range(bits - 1))
    leaf[...] = held[0][:, pl.ds(pl.multiple_of(index * share, share), share)]
    held = (leaf,) + tuple(held[1:])
    for start in range(0, columns, PANEL):
        own, after = slice(start, start + PANEL), slice(start + PANEL, columns)
        last = start + PANEL == columns
        inverses = panel_inverses([gram[own, own] for gram in grams])
        for inverse, source, gram, basis in zip(inverses, held, grams, bases):
            if not last:
                lower = dot3(gram[after, own], inverse, 1, 1)
                gram[after, after] = gram[after, after] - dot3(lower, lower, 1, 1)
            block = dot3(inverse, source[own, :], 1, 0)
            basis[:, own] = block.T * scale
            if not last:
                source[after, :] = source[after, :] - dot3(lower, block, 1, 0)


def bases_of(place, parts, share):
    count = len(parts) // 2
    columns, rows = 2 * parts[0].shape[0], parts[0].shape[1]
    bits = lax.axis_size("samples").bit_length() - 1
    shapes = [(share if m == 0 else rows, columns) for m in range(count)]
    return pl.pallas_call(
        functools.partial(basis_kernel, count=count, bits=bits),
        out_shape=[jax.ShapeDtypeStruct(shape, F32) for shape in shapes],
        in_specs=[SMEM] + [VMEM] * len(parts),
        out_specs=[VMEM] * count,
        scratch_shapes=[pltpu.VMEM((columns, rows), F32)] * count
        + [pltpu.VMEM((columns, columns), F32)] * count
        + [pltpu.VMEM((columns, share), F32)],
        compiler_params=pltpu.CompilerParams(vmem_limit_bytes=BASES_VMEM),
        name="bases",
    )(place, *parts)


def call(kernel, shapes, *operands, **static):
    return pl.pallas_call(
        functools.partial(kernel, **static),
        out_shape=[jax.ShapeDtypeStruct(shape, F32) for shape in shapes],
        in_specs=[SMEM] + [VMEM] * (len(operands) - 1),
        out_specs=[VMEM] * len(shapes),
        compiler_params=pltpu.CompilerParams(vmem_limit_bytes=SMALL_VMEM),
        name=kernel.__name__,
    )(*operands)


def pick(value, indices):
    count, width = value.shape
    lanes = lax.broadcasted_iota(jnp.int32, (width, indices.shape[1]), 0)
    chosen = (lanes == indices).astype(BF16)
    high = value.astype(BF16)
    rest = value - high.astype(F32)
    middle = rest.astype(BF16)
    low = (rest - middle.astype(F32)).astype(BF16)
    found = dot_of(jnp.concatenate([high, middle, low], 0), chosen, 1, 0)
    return found[:count] + (found[count : 2 * count] + found[2 * count :])


def ordered(first, second, swapped):
    return jnp.concatenate(
        [jnp.where(swapped, second, first), jnp.where(swapped, first, second)], 1
    )


def part(ref, index, size):
    return ref[pl.ds(pl.multiple_of(index * size, size), size), :]


def chunk_start(place, bits, other, columns):
    return sum((place[b] ^ other >> b & 1) * (columns >> b + 1) for b in range(bits))


def product_kernel(place, matrix, sketch, pivots, *refs, bits):
    own, other = refs[:2]
    tops = refs[2 : 2 + (1 << bits)]
    rows_held, sketch_held, turned, found, sent, sems = refs[2 + (1 << bits) :]
    leaf, half, columns = matrix.shape[0] // 2, own.shape[0], sketch.shape[1]
    rank = pivots.shape[2]
    sketch_copy = pltpu.make_async_copy(sketch, sketch_held, sems.at[2])
    sketch_copy.start()
    copies = []
    for step in range(2):
        rows = pl.ds(step * leaf, leaf)
        copies.append(pltpu.make_async_copy(matrix.at[rows], rows_held.at[rows], sems.at[step]))
        copies[-1].start()
    sketch_copy.wait()
    turned[...] = sketch_held[...].T
    second = place[0] == 1
    for step, copy in enumerate(copies):
        copy.wait()
        lanes = slice(step * leaf, step * leaf + leaf)
        value = dot_of(turned[...], rows_held[lanes, :], 1, 1)
        near, far = value[:half], value[half:]
        own[:, lanes] = jnp.where(second, far, near)
        other[:, lanes] = jnp.where(second, near, far)
        found[:, step * rank : step * rank + rank] = pick(value, pivots[step])
    sent[...] = pick(found[...], pivots[2])
    for x, top in enumerate(tops):
        size = top.shape[0]
        start = chunk_start(place, bits, x, columns)
        top[...] = sent[pl.ds(pl.multiple_of(start, size), size), :]


def product(place, matrix, sketch, pivots, bits):
    rows, depth = matrix.shape
    columns, rank = sketch.shape[1], pivots.shape[2]
    shapes = [(columns // 2, rows)] * 2 + [(columns >> bits, rank)] * (1 << bits)
    hbm = pl.BlockSpec(memory_space=pltpu.HBM)
    return pl.pallas_call(
        functools.partial(product_kernel, bits=bits),
        out_shape=[jax.ShapeDtypeStruct(shape, F32) for shape in shapes],
        in_specs=[SMEM, hbm, hbm, VMEM],
        out_specs=[VMEM] * len(shapes),
        scratch_shapes=[
            pltpu.VMEM(matrix.shape, BF16),
            pltpu.VMEM(sketch.shape, BF16),
            pltpu.VMEM((columns, depth), BF16),
            pltpu.VMEM((columns, 2 * rank), F32),
            pltpu.VMEM((columns, rank), F32),
            pltpu.SemaphoreType.DMA((3,)),
        ],
        compiler_params=pltpu.CompilerParams(vmem_limit_bytes=PRODUCT_VMEM),
        name="product",
    )(place, matrix, sketch, pivots)


def add_and_halve(place, held, came, own, other, *, bit):
    half = own.shape[0]
    own[...] = part(held, place[bit], half) + part(came, place[bit], half)
    other[...] = part(held, 1 - place[bit], half) + part(came, 1 - place[bit], half)


def add_and_part(place, held, came, own, other, *, bit):
    leaf = own.shape[1]
    for index, out in ((place[bit], own), (1 - place[bit], other)):
        lanes = pl.ds(pl.multiple_of(index * leaf, leaf), leaf)
        out[...] = held[:, lanes] + came[:, lanes]


def add_all(place, *refs):
    refs[-1][...] = sum(ref[...] for ref in refs[1:-1]) + refs[0][...]


def leaf_kernel(place, held, came, pivots, leaf, skeleton, *, bit):
    value = held[...] + came[...]
    leaf[...] = value
    skeleton[...] = pick(value, pivots[place[bit]])


def join_lanes(place, own, came, out, *, bit):
    out[...] = ordered(own[...], came[...], place[bit] == 1)


def join_rows(place, own, came, out, *, bit):
    half = own.shape[0]
    out[pl.ds(pl.multiple_of(place[bit] * half, half), half), :] = own[...]
    out[pl.ds(pl.multiple_of(half - place[bit] * half, half), half), :] = came[...]


def messages(position, node, top, first, second, count):
    rank = top.shape[1]
    root = position % (count // 2) == 0
    first[...] = jnp.where(root, top, node[:, :rank])
    second[...] = jnp.where(root, top, node[:, rank:])


def two_levels(place, own, next_1, next_2, next_3, upper, node, top, first, second, *, at, count):
    position, depth = place[at], count.bit_length() - 1
    odd = position % 2 == 1
    pair = position >> 1
    first_row = (1 << depth - 1) - 2
    mine = ordered(own[...], next_1[...], odd)
    theirs = ordered(next_2[...], next_3[...], odd)
    mine_top = pick(mine, upper[pl.ds(first_row + pair, 1), :])
    theirs_top = pick(theirs, upper[pl.ds(first_row + (pair ^ 1), 1), :])
    both = ordered(mine_top, theirs_top, pair % 2 == 1)
    chosen = jnp.where(odd, mine, both)
    raised = pick(both, upper[pl.ds((1 << depth - 2) - 2 + (position >> 2), 1), :])
    node[...] = chosen
    top[...] = raised
    messages(position, chosen, raised, first, second, count)


def one_level(place, own, came, before, upper, node, top, first, second, *, at, height, count):
    position, depth = place[at], count.bit_length() - 1
    both = ordered(own[...], came[...], (position >> height - 1) % 2 == 1)
    owner = position % (1 << height) == 1 << height - 1
    chosen = jnp.where(owner, both, before[...])
    row = (1 << depth - height) - 2 + (position >> height)
    raised = pick(both, upper[pl.ds(row, 1), :])
    node[...] = chosen
    top[...] = raised
    messages(position, chosen, raised, first, second, count)


def join_node(place, node, top, first, second, third, out, *, at, count, bit):
    root = place[at] % (count // 2) == 0
    right = place[at] == count // 2
    own_root = ordered(top[...], third[...], right)
    half = node.shape[0]
    mine = pl.ds(pl.multiple_of(place[bit] * half, half), half)
    theirs = pl.ds(pl.multiple_of(half - place[bit] * half, half), half)
    out[mine, :] = jnp.where(root, own_root, node[...])
    out[theirs, :] = ordered(first[...], second[...], right)


def exchange(block, other):
    count = lax.axis_size("samples")
    return lax.ppermute(block, "samples", [(s, s ^ other) for s in range(count)])


def swap(block, bit):
    return exchange(block, 1 << bit)


def climb(place, current, upper, at, bits):
    count, shares = lax.axis_size("rows"), lax.axis_size("samples")
    depth = count.bit_length() - 1
    wide, narrow = (current.shape[0], 2 * current.shape[1]), current.shape
    came = [
        lax.ppermute(current, "rows", [(d, d ^ step) for d in range(count)]) for step in (1, 2, 3)
    ]
    shapes = [wide, narrow, narrow, narrow]
    node, top, first, second = call(
        two_levels, shapes, place, current, *came, upper, at=at, count=count
    )
    for height in range(3, depth):
        partner = lax.ppermute(top, "rows", [(d, d ^ 1 << height - 1) for d in range(count)])
        node, top, first, second = call(
            one_level, shapes, place, top, partner, node, upper, at=at, height=height, count=count
        )
    bit = bits - 1
    far = count // 2
    across, other_side, along = [], [], []
    for d in range(count):
        for s in range(shares):
            source = d * shares + s
            turned = s ^ 1 << bit
            across.append((source, d * shares + turned))
            if d % far == 0:
                other_side.append((source, (d ^ far) * shares + turned))
                along.append((source, (d ^ far) * shares + s))
            else:
                other_side.append((source, d * shares + turned))
    axes = ("rows", "samples")
    first = lax.ppermute(first, axes, across)
    second = lax.ppermute(second, axes, other_side)
    third = lax.ppermute(top, axes, along)
    half = (2 * wide[0], wide[1])
    return call(
        join_node, [half], place, node, top, first, second, third, at=at, count=count, bit=bit
    )[0]


def on_device(matrix_block, sketch_matrix, local_pivots, upper_pivots):
    shares = lax.axis_size("samples")
    bits = shares.bit_length() - 1
    share, position = lax.axis_index("samples"), lax.axis_index("rows")
    place = jnp.stack([share >> b & 1 for b in range(bits)] + [position]).astype(jnp.int32)
    pivots = jnp.transpose(local_pivots, (1, 0, 2))
    rows, rank = matrix_block.shape[0], pivots.shape[2]

    own, other, *tops = product(place, matrix_block, sketch_matrix, pivots, bits)
    tops = tops[:1] + [exchange(top, x) for x, top in enumerate(tops) if x > 0]
    came = exchange(other, 1)
    own, came, tops = lax.optimization_barrier((own, came, tops))
    for bit in range(1, bits - 1):
        half = (own.shape[0] // 2, rows)
        own, other = call(add_and_halve, [half] * 2, place, own, came, bit=bit)
        came = swap(other, bit)
    last = bits - 1
    leaf_shape = (own.shape[0], rows // 2)
    own, other = call(add_and_part, [leaf_shape] * 2, place, own, came, bit=last)
    came = swap(other, last)

    top = call(add_all, [tops[0].shape], place, *tops)[0]
    node = climb(place, top, upper_pivots, bits, bits)

    leaf, skeleton = call(
        leaf_kernel, [leaf_shape, (leaf_shape[0], rank)], place, own, came, pivots, bit=last
    )
    skeleton_came = swap(skeleton, last)
    stacked = call(
        join_lanes, [(leaf_shape[0], 2 * rank)], place, skeleton, skeleton_came, bit=last
    )[0]
    held = [leaf, stacked, node]
    for bit in range(bits - 2, 0, -1):
        whole = (2 * held[0].shape[0], held[0].shape[1])
        held = [call(join_rows, [whole], place, one, swap(one, bit), bit=bit)[0] for one in held]
    parts = []
    for one in held:
        parts += [one, swap(one, 0)]
    return tuple(bases_of(place, parts, rows // shares))


def solution(mesh):
    in_specs = (P("rows", "samples"), P("samples", None), P("rows", None, None), P())
    out_specs = (P(("rows", "samples"), None), P("rows", None), P("rows", None))
    return jax.shard_map(
        on_device, mesh=mesh, in_specs=in_specs, out_specs=out_specs, check_vma=False
    )
```

time: 166 us -> 72.8 us (0.44)
  waiting for transfers between devices: 77 us -> 17.2 us
  other arithmetic: 21.2 us -> 0.62 us
  local copies, waits for them, and re-layouts: 17.4 us -> 2.04 us
  between operations: 14.2 us -> 0.75 us
  Pallas kernels: 23.4 us -> 35.2 us
  starting transfers between devices: 5.4 us -> 16.8 us
  matrix products: 6.47 us -> 0 us
    psum x1 -> x0, waiting for transfers between devices: 43.1 us -> none  [on_device(): summed = lax.psum(partial_value, 'samples')]
    ppermute x3 -> x15, waiting for transfers between devices: 33.8 us -> 17.2 us  [the longest x9 12.2 us: exchange(): lax.ppermute(block, 'samples', [(s, s ^ other) for s in range(count)])]
    select_n x13 -> x0, other arithmetic: 13.7 us -> none  [the longest x9 8.49 us: select_rows(): return jnp.take(matrix_rows, indices, axis=0)]
    gather x5 -> x0, local copies, waits for them, and re-layouts: 12.6 us -> none  [select_rows(): return jnp.take(matrix_rows, indices, axis=0)]
    pallas_call x1 -> x8, Pallas kernels: 23.4 us -> 35.2 us  [the longest x1 23.1 us: bases_of(): pl.pallas_call(functools.partial(basis_kernel, count=count, bits=bits), o...]
    ppermute x3 -> x15, starting transfers between devices: 5.37 us -> 16.8 us  [the longest x9 6.69 us: exchange(): lax.ppermute(block, 'samples', [(s, s ^ other) for s in range(count)])]
    dot_general x1 -> x0, matrix products: 6.47 us -> none  [on_device(): jnp.dot(matrix_block, sketch_matrix, preferred_element_type=jnp.float32)]
    concatenate x3 -> x0, other arithmetic: 2.91 us -> none  [the longest x2 1.86 us: climb_tree(): stacked = jnp.concatenate([left_part, right_part], 0)]
  transfers between devices with their start and end apart: 4 -> 15, of which waited for: 4 -> 8; matrix products, arithmetic and copies ran while one was open for 2% -> 0% of each run, Pallas kernels for 0% -> 5%
where the time goes in v1:
time: 72.8 us; the launch traced here: 72.6 us
  Pallas kernels  35.2 us (48%)
  waiting for transfers between devices  17.2 us (24%)
  starting transfers between devices  16.8 us (23%)
  local copies, waits for them, and re-layouts  2.04 us (3%)
  between operations  0.75 us (1%)
    pallas_call x1, Pallas kernels, bases_of(): pl.pallas_call(functools.partial(basis_kernel, count=count, bits=bits), o...  23.1 us
    ppermute x9, waiting for transfers between devices, exchange(): lax.ppermute(block, 'samples', [(s, s ^ other) for s in range(count)])  12.2 us
    pallas_call x1, Pallas kernels, product(): pl.pallas_call(functools.partial(product_kernel, bits=bits), out_shape=[j...  7.6 us
    ppermute x9, starting transfers between devices, exchange(): lax.ppermute(block, 'samples', [(s, s ^ other) for s in range(count)])  6.69 us
    pallas_call x6, Pallas kernels, call(): pl.pallas_call(functools.partial(kernel, **static), out_shape=[jax.ShapeD...  4.46 us
    ppermute x1, waiting for transfers between devices, climb(): third = lax.ppermute(top, axes, along)  3.63 us
    ppermute x3, starting transfers between devices, climb(): lax.ppermute(current, 'rows', [(d, d ^ step) for d in range(count)])  3.55 us
    ppermute x1, starting transfers between devices, climb(): second = lax.ppermute(second, axes, other_side)  3.49 us
  transfers between devices with their start and end apart: 15, of which 8 were waited for; matrix products, arithmetic and copies ran while one was open for 0% of the time, Pallas kernels for 5%

profile of v1, /device:TPU:0, one launch (start us, length us, event | category | flops | bytes accessed | tf_op | source)
XLA Modules:
  0.0 72.6 jit_solution(11613413521487298492)
XLA Ops:
  0.6 0.0 copy-start.3
  0.6 0.0 copy-start.4
  0.7 0.6 pad_add_fusion.place.refs_0_
  1.3 0.0 copy-start.2
  1.3 7.6 %product.1 = (f32[192,1024]{1,0:T(8,128)}, f32[192,1024]{1,0:T(8,128)}, f32[96,256]{1,0:T(8,128)}, f32[96,256]{1,0:T(8,128)}, f32[96,256]{1,0:T(8,128)}, /*index=5*/f32[96,256]{1,0:T(8,128)}) custom-call(s32[3]{0:T(128)} %pad_add_fusion.place.refs_0_, bf16[1024,2560]{1,0:T(8,128)(2,1)} %matrix.1, bf16[2560,384]{1,0:T(8,128)(2,1)} %sketch.1, s32[3,1,256]{2,1,0:T(1,128)} %bitcast.4), custom_call_target="tpu_custom_call" | custom-call | tf_op jit(solution)/shard_map/product/pallas_call | solution.py:239
  8.9 0.5 collective-permute-start
  9.4 0.1 collective-permute-start.1
  9.5 2.9 %collective-permute-start.2 = (f32[96,256]{1,0:T(8,128)}, f32[96,256]{1,0:T(8,128)S(1)}, u32[]{:S(2)}, u32[]{:S(2)}) collective-permute-start(f32[96,256]{1,0:T(8,128)} %get-tuple-element.27), channel_id=1, source_target_pairs={{0,2},{1,3},{2,0},{3,1},{4,6},{5,7},{6,4},{7,5},{8,10},{9,11},{10,... | collective-permute-start | bytes 294920 | tf_op jit(solution)/shard_map/ppermute | solution.py:339
  12.4 0.0 collective-permute-start.3
  12.4 0.0 collective-permute-done.1.refs_1_
  12.4 3.5 %collective-permute-done.2.refs_2_ = f32[96,256]{1,0:T(8,128)S(1)} collective-permute-done((f32[96,256]{1,0:T(8,128)}, f32[96,256]{1,0:T(8,128)S(1)}, u32[]{:S(2)}, u32[]{:S(2)}) %collective-permute-start.2) | collective-permute-done | bytes 98336 | tf_op jit(solution)/shard_map/ppermute | solution.py:339
  15.9 1.9 %collective-permute-done.3.refs_3_ = f32[96,256]{1,0:T(8,128)S(1)} collective-permute-done((f32[96,256]{1,0:T(8,128)}, f32[96,256]{1,0:T(8,128)S(1)}, u32[]{:S(2)}, u32[]{:S(2)}) %collective-permute-start.3) | collective-permute-done | bytes 98336 | tf_op jit(solution)/shard_map/ppermute | solution.py:339
  17.7 0.0 collective-permute-done.came
  17.8 0.0 copy-done.2
  17.8 0.0 copy-start
  17.8 1.1 %copy-done = f32[192,1024]{1,0:T(8,128)S(1)} copy-done((f32[192,1024]{1,0:T(8,128)S(1)}, f32[192,1024]{1,0:T(8,128)}, u32[]{:S(2)}) %copy-start) | copy-done | bytes 786456
  18.9 0.6 add_and_part.1
  19.5 0.9 %collective-permute-start.4 = (f32[192,512]{1,0:T(8,128)S(1)}, f32[192,512]{1,0:T(8,128)S(1)}, u32[]{:S(2)}, u32[]{:S(2)}) collective-permute-start(f32[192,512]{1,0:T(8,128)S(1)} %get-tuple-element.32), channel_id=1, source_target_pairs={{0,2},{1,3},{2,0},{3,1},{4,6},{5,7},{6,4},{7,5},{8,10},{9,11},{10,... | collective-permute-start | bytes 1179656 | tf_op jit(solution)/shard_map/ppermute | solution.py:339
  20.5 0.9 %copy-done.1 = f32[96,256]{1,0:T(8,128)S(1)} copy-done((f32[96,256]{1,0:T(8,128)S(1)}, f32[96,256]{1,0:T(8,128)}, u32[]{:S(2)}) %copy-start.1) | copy-done | bytes 98328
  21.3 0.6 add_all.1.own
  21.9 2.6 %collective-permute-start.10 = (f32[96,256]{1,0:T(8,128)S(1)}, f32[96,256]{1,0:T(8,128)S(1)}, u32[]{:S(2)}, u32[]{:S(2)}) collective-permute-start(f32[96,256]{1,0:T(8,128)S(1)} %add_all.1.own), channel_id=1, source_target_pairs={{0,12},{4,8},{8,4},{12,0},{16,28},{20,24},{24,20},{28,16},{1,13},{... | collective-permute-start | bytes 294920 | tf_op jit(solution)/shard_map/ppermute | solution.py:351
  24.5 0.4 collective-permute-start.9
  25.0 0.5 collective-permute-start.8
  25.5 5.2 %collective-permute-done.4.came = f32[192,512]{1,0:T(8,128)S(1)} collective-permute-done((f32[192,512]{1,0:T(8,128)S(1)}, f32[192,512]{1,0:T(8,128)S(1)}, u32[]{:S(2)}, u32[]{:S(2)}) %collective-permute-start.4) | collective-permute-done | bytes 393248 | tf_op jit(solution)/shard_map/ppermute | solution.py:339
  30.7 0.0 copy-done.3
  30.7 0.9 %leaf_kernel.1 = (f32[192,512]{1,0:T(8,128)S(1)}, f32[192,256]{1,0:T(8,128)S(1)}) custom-call(s32[3]{0:T(128)S(1)} %copy-done.2, f32[192,512]{1,0:T(8,128)S(1)} %get-tuple-element.31.held, f32[192,512]{1,0:T(8,128)S(1)} %collective-permute-done.4.came, s32[3,1,256]{2,1,0:T(1,128)S(1)} %bitcast.5), custom_call_target="tpu_custom_call" | custom-call | tf_op jit(solution)/shard_map/leaf_kernel/pallas_call | solution.py:167
  31.6 1.5 %collective-permute-start.6 = (f32[192,256]{1,0:T(8,128)S(1)}, f32[192,256]{1,0:T(8,128)S(1)}, u32[]{:S(2)}, u32[]{:S(2)}) collective-permute-start(f32[192,256]{1,0:T(8,128)S(1)} %get-tuple-element.34.own), channel_id=1, source_target_pairs={{0,2},{1,3},{2,0},{3,1},{4,6},{5,7},{6,4},{7,5},{8,10},{9,11},{10,... | collective-permute-start | bytes 589832 | tf_op jit(solution)/shard_map/ppermute | solution.py:339
  33.1 0.0 collective-permute-done.10.next_3
  33.2 0.0 collective-permute-done.9.next_2
  33.2 0.0 collective-permute-done.8.next_1
  33.2 0.0 copy-done.4
  33.2 1.2 %two_levels.1 = (f32[96,512]{1,0:T(8,128)S(1)}, f32[96,256]{1,0:T(8,128)S(1)}, f32[96,256]{1,0:T(8,128)S(1)}, f32[96,256]{1,0:T(8,128)S(1)}) custom-call(s32[3]{0:T(128)S(1)} %copy-done.2, f32[96,256]{1,0:T(8,128)S(1)} %add_all.1.own, f32[96,256]{1,0:T(8,128)S(1)} %collective-permute-done.8.next_1, f32[96,256]{1,0:T(8,128)S(1)} %collective-permute-done.9.next_2, ...), custom_call_target="tpu_custom_call" | custom-call | tf_op jit(solution)/shard_map/two_levels/pallas_call | solution.py:167
  34.4 0.6 collective-permute-start.11
  35.0 3.5 %collective-permute-start.12 = (f32[96,256]{1,0:T(8,128)S(1)}, f32[96,256]{1,0:T(8,128)S(1)}, u32[]{:S(2)}, u32[]{:S(2)}) collective-permute-start(f32[96,256]{1,0:T(8,128)S(1)} %get-tuple-element.42), channel_id=1, source_target_pairs={{0,18},{1,19},{2,16},{3,17},{4,6},{5,7},{6,4},{7,5},{8,10},{9,11},... | collective-permute-start | bytes 294920 | tf_op jit(solution)/shard_map/ppermute | solution.py:377
  38.5 2.4 %collective-permute-start.13 = (f32[96,256]{1,0:T(8,128)S(1)}, f32[96,256]{1,0:T(8,128)S(1)}, u32[]{:S(2)}, u32[]{:S(2)}) collective-permute-start(f32[96,256]{1,0:T(8,128)S(1)} %get-tuple-element.40.top), channel_id=1, source_target_pairs={{0,16},{1,17},{2,18},{3,19},{16,0},{17,1},{18,2},{19,3}} | collective-permute-start | bytes 294920 | tf_op jit(solution)/shard_map/ppermute | solution.py:378
  40.9 1.3 %collective-permute-done.11.first = f32[96,256]{1,0:T(8,128)S(1)} collective-permute-done((f32[96,256]{1,0:T(8,128)S(1)}, f32[96,256]{1,0:T(8,128)S(1)}, u32[]{:S(2)}, u32[]{:S(2)}) %collective-permute-start.11) | collective-permute-done | bytes 98336 | tf_op jit(solution)/shard_map/ppermute | solution.py:376
  42.3 0.0 collective-permute-done.12.second
  42.3 3.6 %collective-permute-done.13.third = f32[96,256]{1,0:T(8,128)S(1)} collective-permute-done((f32[96,256]{1,0:T(8,128)S(1)}, f32[96,256]{1,0:T(8,128)S(1)}, u32[]{:S(2)}, u32[]{:S(2)}) %collective-permute-start.13) | collective-permute-done | bytes 98336 | tf_op jit(solution)/shard_map/ppermute | solution.py:378
  45.9 0.6 join_node.1.refs_5_
  46.5 0.1 collective-permute-start.14
  46.6 0.5 collective-permute-start.5
  47.1 0.0 collective-permute-done.6.came
  47.1 0.6 join_lanes.1.refs_3_
  47.7 0.1 collective-permute-start.7
  47.8 0.5 collective-permute-done.14.refs_6_
  48.3 0.6 collective-permute-done.5.refs_2_
  48.8 0.6 collective-permute-done.7.refs_4_
  49.4 23.1 %bases.1 = (f32[256,384]{1,0:T(8,128)}, f32[512,384]{1,0:T(8,128)}, f32[512,384]{1,0:T(8,128)}) custom-call(s32[3]{0:T(128)S(1)} %copy-done.2, f32[192,512]{1,0:T(8,128)S(1)} %get-tuple-element.33.refs_1_, f32[192,512]{1,0:T(8,128)S(1)} %collective-permute-done.5.refs_2_, f32[192,512]{1,0:T(8,128)S(1)} %join_lanes.1.refs_3_, ...), custom_call_target="tpu_custom_call" | custom-call | tf_op jit(solution)/shard_map/bases/pallas_call | solution.py:153
  (1 shorter events, 0.0 us)
Async XLA Ops:
  0.6 30.1 %copy-start.3 = (s32[1,3,256]{2,0,1:T(1,128)S(1)}, s32[1,3,256]{2,0,1:T(1,128)}, u32[]{:S(2)}) copy-start(s32[1,3,256]{2,0,1:T(1,128)} %param.6) | copy-start | bytes 9220
  0.6 32.5 %copy-start.4 = (s32[6,256]{1,0:T(8,128)S(1)}, s32[6,256]{1,0:T(8,128)}, u32[]{:S(2)}) copy-start(s32[6,256]{1,0:T(8,128)} %upper.1) | copy-start | bytes 18436
  1.3 16.5 %copy-start.2 = (s32[3]{0:T(128)S(1)}, s32[3]{0:T(128)}, u32[]{:S(2)}) copy-start(s32[3]{0:T(128)} %pad_add_fusion.place.refs_0_) | copy-start | bytes 40
  8.9 8.9 %collective-permute-start = (f32[192,1024]{1,0:T(8,128)}, f32[192,1024]{1,0:T(8,128)S(1)}, u32[]{:S(2)}, u32[]{:S(2)}) collective-permute-start(f32[192,1024]{1,0:T(8,128)} %get-tuple-element.24), channel_id=1, source_target_pairs={{0,1},{1,0},{2,3},{3,2},{4,5},{5,4},{6,7},{7,6},{8,9},{9,8},{10,11... | collective-permute-start | bytes 2359304 | tf_op jit(solution)/shard_map/ppermute | solution.py:339
  9.4 3.0 %collective-permute-start.1 = (f32[96,256]{1,0:T(8,128)}, f32[96,256]{1,0:T(8,128)S(1)}, u32[]{:S(2)}, u32[]{:S(2)}) collective-permute-start(f32[96,256]{1,0:T(8,128)} %get-tuple-element.26), channel_id=1, source_target_pairs={{0,1},{1,0},{2,3},{3,2},{4,5},{5,4},{6,7},{7,6},{8,9},{9,8},{10,11... | collective-permute-start | bytes 294920 | tf_op jit(solution)/shard_map/ppermute | solution.py:339
  9.5 6.4 %collective-permute-start.2 = (f32[96,256]{1,0:T(8,128)}, f32[96,256]{1,0:T(8,128)S(1)}, u32[]{:S(2)}, u32[]{:S(2)}) collective-permute-start(f32[96,256]{1,0:T(8,128)} %get-tuple-element.27), channel_id=1, source_target_pairs={{0,2},{1,3},{2,0},{3,1},{4,6},{5,7},{6,4},{7,5},{8,10},{9,11},{10,... | collective-permute-start | bytes 294920 | tf_op jit(solution)/shard_map/ppermute | solution.py:339
  12.4 5.4 %collective-permute-start.3 = (f32[96,256]{1,0:T(8,128)}, f32[96,256]{1,0:T(8,128)S(1)}, u32[]{:S(2)}, u32[]{:S(2)}) collective-permute-start(f32[96,256]{1,0:T(8,128)} %get-tuple-element.28), channel_id=1, source_target_pairs={{0,3},{1,2},{2,1},{3,0},{4,7},{5,6},{6,5},{7,4},{8,11},{9,10},{10,... | collective-permute-start | bytes 294920 | tf_op jit(solution)/shard_map/ppermute | solution.py:339
  17.8 1.1 %copy-start = (f32[192,1024]{1,0:T(8,128)S(1)}, f32[192,1024]{1,0:T(8,128)}, u32[]{:S(2)}) copy-start(f32[192,1024]{1,0:T(8,128)} %get-tuple-element.29.held) | copy-start | bytes 2359300
  19.5 11.2 %collective-permute-start.4 = (f32[192,512]{1,0:T(8,128)S(1)}, f32[192,512]{1,0:T(8,128)S(1)}, u32[]{:S(2)}, u32[]{:S(2)}) collective-permute-start(f32[192,512]{1,0:T(8,128)S(1)} %get-tuple-element.32), channel_id=1, source_target_pairs={{0,2},{1,3},{2,0},{3,1},{4,6},{5,7},{6,4},{7,5},{8,10},{9,11},{10,... | collective-permute-start | bytes 1179656 | tf_op jit(solution)/shard_map/ppermute | solution.py:339
  20.5 0.9 %copy-start.1 = (f32[96,256]{1,0:T(8,128)S(1)}, f32[96,256]{1,0:T(8,128)}, u32[]{:S(2)}) copy-start(f32[96,256]{1,0:T(8,128)} %get-tuple-element.35.refs_0_) | copy-start | bytes 294916
  21.9 11.2 %collective-permute-start.10 = (f32[96,256]{1,0:T(8,128)S(1)}, f32[96,256]{1,0:T(8,128)S(1)}, u32[]{:S(2)}, u32[]{:S(2)}) collective-permute-start(f32[96,256]{1,0:T(8,128)S(1)} %add_all.1.own), channel_id=1, source_target_pairs={{0,12},{4,8},{8,4},{12,0},{16,28},{20,24},{24,20},{28,16},{1,13},{... | collective-permute-start | bytes 294920 | tf_op jit(solution)/shard_map/ppermute | solution.py:351
  24.5 8.6 %collective-permute-start.9 = (f32[96,256]{1,0:T(8,128)S(1)}, f32[96,256]{1,0:T(8,128)S(1)}, u32[]{:S(2)}, u32[]{:S(2)}) collective-permute-start(f32[96,256]{1,0:T(8,128)S(1)} %add_all.1.own), channel_id=1, source_target_pairs={{0,8},{4,12},{8,0},{12,4},{16,24},{20,28},{24,16},{28,20},{1,9},{5... | collective-permute-start | bytes 294920 | tf_op jit(solution)/shard_map/ppermute | solution.py:351
  25.0 8.2 %collective-permute-start.8 = (f32[96,256]{1,0:T(8,128)S(1)}, f32[96,256]{1,0:T(8,128)S(1)}, u32[]{:S(2)}, u32[]{:S(2)}) collective-permute-start(f32[96,256]{1,0:T(8,128)S(1)} %add_all.1.own), channel_id=1, source_target_pairs={{0,4},{4,0},{8,12},{12,8},{16,20},{20,16},{24,28},{28,24},{1,5},{5... | collective-permute-start | bytes 294920 | tf_op jit(solution)/shard_map/ppermute | solution.py:351
  31.6 15.5 %collective-permute-start.6 = (f32[192,256]{1,0:T(8,128)S(1)}, f32[192,256]{1,0:T(8,128)S(1)}, u32[]{:S(2)}, u32[]{:S(2)}) collective-permute-start(f32[192,256]{1,0:T(8,128)S(1)} %get-tuple-element.34.own), channel_id=1, source_target_pairs={{0,2},{1,3},{2,0},{3,1},{4,6},{5,7},{6,4},{7,5},{8,10},{9,11},{10,... | collective-permute-start | bytes 589832 | tf_op jit(solution)/shard_map/ppermute | solution.py:339
  34.4 7.9 %collective-permute-start.11 = (f32[96,256]{1,0:T(8,128)S(1)}, f32[96,256]{1,0:T(8,128)S(1)}, u32[]{:S(2)}, u32[]{:S(2)}) collective-permute-start(f32[96,256]{1,0:T(8,128)S(1)} %get-tuple-element.41), channel_id=1, source_target_pairs={{0,2},{1,3},{2,0},{3,1},{4,6},{5,7},{6,4},{7,5},{8,10},{9,11},{10,... | collective-permute-start | bytes 294920 | tf_op jit(solution)/shard_map/ppermute | solution.py:376
  35.0 7.3 %collective-permute-start.12 = (f32[96,256]{1,0:T(8,128)S(1)}, f32[96,256]{1,0:T(8,128)S(1)}, u32[]{:S(2)}, u32[]{:S(2)}) collective-permute-start(f32[96,256]{1,0:T(8,128)S(1)} %get-tuple-element.42), channel_id=1, source_target_pairs={{0,18},{1,19},{2,16},{3,17},{4,6},{5,7},{6,4},{7,5},{8,10},{9,11},... | collective-permute-start | bytes 294920 | tf_op jit(solution)/shard_map/ppermute | solution.py:377
  38.5 7.4 %collective-permute-start.13 = (f32[96,256]{1,0:T(8,128)S(1)}, f32[96,256]{1,0:T(8,128)S(1)}, u32[]{:S(2)}, u32[]{:S(2)}) collective-permute-start(f32[96,256]{1,0:T(8,128)S(1)} %get-tuple-element.40.top), channel_id=1, source_target_pairs={{0,16},{1,17},{2,18},{3,19},{16,0},{17,1},{18,2},{19,3}} | collective-permute-start | bytes 294920 | tf_op jit(solution)/shard_map/ppermute | solution.py:378
  46.5 1.8 %collective-permute-start.14 = (f32[192,512]{1,0:T(8,128)S(1)}, f32[192,512]{1,0:T(8,128)S(1)}, u32[]{:S(2)}, u32[]{:S(2)}) collective-permute-start(f32[192,512]{1,0:T(8,128)S(1)} %join_node.1.refs_5_), channel_id=1, source_target_pairs={{0,1},{1,0},{2,3},{3,2},{4,5},{5,4},{6,7},{7,6},{8,9},{9,8},{10,11... | collective-permute-start | bytes 1179656 | tf_op jit(solution)/shard_map/ppermute | solution.py:339
  46.6 2.3 %collective-permute-start.5 = (f32[192,512]{1,0:T(8,128)S(1)}, f32[192,512]{1,0:T(8,128)S(1)}, u32[]{:S(2)}, u32[]{:S(2)}) collective-permute-start(f32[192,512]{1,0:T(8,128)S(1)} %get-tuple-element.33.refs_1_), channel_id=1, source_target_pairs={{0,1},{1,0},{2,3},{3,2},{4,5},{5,4},{6,7},{7,6},{8,9},{9,8},{10,11... | collective-permute-start | bytes 1179656 | tf_op jit(solution)/shard_map/ppermute | solution.py:339
  47.7 1.8 %collective-permute-start.7 = (f32[192,512]{1,0:T(8,128)S(1)}, f32[192,512]{1,0:T(8,128)S(1)}, u32[]{:S(2)}, u32[]{:S(2)}) collective-permute-start(f32[192,512]{1,0:T(8,128)S(1)} %join_lanes.1.refs_3_), channel_id=1, source_target_pairs={{0,1},{1,0},{2,3},{3,2},{4,5},{5,4},{6,7},{7,6},{8,9},{9,8},{10,11... | collective-permute-start | bytes 1179656 | tf_op jit(solution)/shard_map/ppermute | solution.py:339

commit v2 on v1

--- a/solution.py
+++ b/solution.py
@@ -13,7 +13,7 @@
 PANEL = 128
 STRIP = 32
 AHEAD = 5
-PRODUCT_VMEM = 61 << 20
+PRODUCT_VMEM = 51 << 20
 SMALL_VMEM = 12 << 20
 BASES_VMEM = 24 << 20
 VMEM = pl.BlockSpec(memory_space=pltpu.VMEM)
@@ -260,7 +260,7 @@
     other[...] = part(held, 1 - place[bit], half) + part(came, 1 - place[bit], half)
 
 
-def add_and_part(place, held, came, own, other, *, bit):
+def add_and_part(place, held, came, gate, own, other, *, bit):
     leaf = own.shape[1]
     for index, out in ((place[bit], own), (1 - place[bit], other)):
         lanes = pl.ds(pl.multiple_of(index * leaf, leaf), leaf)
@@ -271,7 +271,7 @@
     refs[-1][...] = sum(ref[...] for ref in refs[1:-1]) + refs[0][...]
 
 
-def leaf_kernel(place, held, came, pivots, leaf, skeleton, *, bit):
+def leaf_kernel(place, held, came, pivots, gate, leaf, skeleton, *, bit):
     value = held[...] + came[...]
     leaf[...] = value
     skeleton[...] = pick(value, pivots[place[bit]])
@@ -343,7 +343,7 @@
     return exchange(block, 1 << bit)
 
 
-def climb(place, current, upper, at, bits):
+def climb(place, current, upper, at, bits, aside):
     count, shares = lax.axis_size("rows"), lax.axis_size("samples")
     depth = count.bit_length() - 1
     wide, narrow = (current.shape[0], 2 * current.shape[1]), current.shape
@@ -377,9 +377,13 @@
     second = lax.ppermute(second, axes, other_side)
     third = lax.ppermute(top, axes, along)
     half = (2 * wide[0], wide[1])
-    return call(
+    extra = aside(node)
+    leaf_came = extra[-1]
+    first, second, third, leaf_came = lax.optimization_barrier((first, second, third, leaf_came))
+    joined = call(
         join_node, [half], place, node, top, first, second, third, at=at, count=count, bit=bit
     )[0]
+    return joined, extra[:-1] + (leaf_came,)
 
 
 def on_device(matrix_block, sketch_matrix, local_pivots, upper_pivots):
@@ -393,23 +397,27 @@
     own, other, *tops = product(place, matrix_block, sketch_matrix, pivots, bits)
     tops = tops[:1] + [exchange(top, x) for x, top in enumerate(tops) if x > 0]
     came = exchange(other, 1)
-    own, came, tops = lax.optimization_barrier((own, came, tops))
     for bit in range(1, bits - 1):
         half = (own.shape[0] // 2, rows)
         own, other = call(add_and_halve, [half] * 2, place, own, came, bit=bit)
         came = swap(other, bit)
+    top = call(add_all, [tops[0].shape], place, *tops)[0]
     last = bits - 1
     leaf_shape = (own.shape[0], rows // 2)
-    own, other = call(add_and_part, [leaf_shape] * 2, place, own, came, bit=last)
+    own, other = call(add_and_part, [leaf_shape] * 2, place, own, came, top, bit=last)
     came = swap(other, last)
 
-    top = call(add_all, [tops[0].shape], place, *tops)[0]
-    node = climb(place, top, upper_pivots, bits, bits)
-
-    leaf, skeleton = call(
-        leaf_kernel, [leaf_shape, (leaf_shape[0], rank)], place, own, came, pivots, bit=last
+    def leaf_part(gate):
+        leaf, skeleton = call(
+            leaf_kernel,
+            [leaf_shape, (leaf_shape[0], rank)],
+            place, own, came, pivots, gate, bit=last,
+        )
+        return leaf, skeleton, swap(skeleton, last), exchange(leaf, 1)
+
+    node, (leaf, skeleton, skeleton_came, leaf_came) = climb(
+        place, top, upper_pivots, bits, bits, leaf_part
     )
-    skeleton_came = swap(skeleton, last)
     stacked = call(
         join_lanes, [(leaf_shape[0], 2 * rank)], place, skeleton, skeleton_came, bit=last
     )[0]
@@ -417,9 +425,10 @@
     for bit in range(bits - 2, 0, -1):
         whole = (2 * held[0].shape[0], held[0].shape[1])
         held = [call(join_rows, [whole], place, one, swap(one, bit), bit=bit)[0] for one in held]
-    parts = []
-    for one in held:
-        parts += [one, swap(one, 0)]
+    came = [exchange(one, 1) for one in held]
+    if bits == 2:
+        came[0] = leaf_came
+    parts = [half for pair in zip(held, came) for half in pair]
     return tuple(bases_of(place, parts, rows // shares))
 
 

time: 72.8 us -> 68.9 us (0.946)
  local copies, waits for them, and re-layouts: 2.04 us -> 0.69 us
  Pallas kernels: 35.2 us -> 34.3 us
    ppermute x3, waiting for transfers between devices: 0.01 us -> 4.7 us  [climb(): lax.ppermute(current, 'rows', [(d, d ^ step) for d in range(count)])]
    ppermute x9, waiting for transfers between devices: 12.2 us -> 9.55 us  [exchange(): lax.ppermute(block, 'samples', [(s, s ^ other) for s in range(count)])]
    ppermute x1, waiting for transfers between devices: 3.63 us -> 1.44 us  [climb(): third = lax.ppermute(top, axes, along)]
    unnamed x10 -> x4, local copies, waits for them, and re-layouts: 2.04 us -> 0.69 us
    pallas_call x1, Pallas kernels: 7.6 us -> 6.69 us  [product(): pl.pallas_call(functools.partial(product_kernel, bits=bits), out_shape=[j...]
  transfers between devices with their start and end apart: 15 -> 15, of which waited for: 8 -> 9; matrix products, arithmetic and copies ran while one was open for 0% -> 0% of each run, Pallas kernels for 5% -> 4%
where the time goes in v2:
time: 68.9 us; the launch traced here: 68.6 us
  Pallas kernels  34.3 us (50%)
  waiting for transfers between devices  16.7 us (24%)
  starting transfers between devices  16.1 us (23%)
  between operations  0.75 us (1%)
  local copies, waits for them, and re-layouts  0.69 us (1%)
    pallas_call x1, Pallas kernels, bases_of(): pl.pallas_call(functools.partial(basis_kernel, count=count, bits=bits), o...  23.1 us
    ppermute x9, waiting for transfers between devices, exchange(): lax.ppermute(block, 'samples', [(s, s ^ other) for s in range(count)])  9.55 us
    pallas_call x1, Pallas kernels, product(): pl.pallas_call(functools.partial(product_kernel, bits=bits), out_shape=[j...  6.69 us
    ppermute x9, starting transfers between devices, exchange(): lax.ppermute(block, 'samples', [(s, s ^ other) for s in range(count)])  6.19 us
    ppermute x3, waiting for transfers between devices, climb(): lax.ppermute(current, 'rows', [(d, d ^ step) for d in range(count)])  4.7 us
    pallas_call x6, Pallas kernels, call(): pl.pallas_call(functools.partial(kernel, **static), out_shape=[jax.ShapeD...  4.47 us
    ppermute x3, starting transfers between devices, climb(): lax.ppermute(current, 'rows', [(d, d ^ step) for d in range(count)])  3.49 us
    ppermute x1, starting transfers between devices, climb(): second = lax.ppermute(second, axes, other_side)  3.48 us
  transfers between devices with their start and end apart: 15, of which 9 were waited for; matrix products, arithmetic and copies ran while one was open for 0% of the time, Pallas kernels for 4%

profile of v2, /device:TPU:0, one launch (start us, length us, event | category | flops | bytes accessed | tf_op | source)
XLA Modules:
  0.0 68.6 jit_solution(2541793937813191617)
XLA Ops:
  0.6 0.0 copy-start.1
  0.6 0.1 pad_add_fusion.place.refs_0_
  0.7 0.0 copy-start
  0.7 0.7 copy-done
  1.4 6.7 %product.1 = (f32[192,1024]{1,0:T(8,128)S(1)}, f32[192,1024]{1,0:T(8,128)S(1)}, f32[96,256]{1,0:T(8,128)S(1)}, f32[96,256]{1,0:T(8,128)S(1)}, f32[96,256]{1,0:T(8,128)S(1)}, /*index=5*/f32[96,256]{1,0:T(8,128)S(1)}) custom-call(s32[3]{0:T(128)S(1)} %pad_add_fusion.place.refs_0_, bf16[1024,2560]{1,0:T(8,128)(2,1)} %matrix.1, bf16[2560,384]{1,0:T(8,128)(2,1)} %sketch.1, ...), custom_call_target="tpu_custom_call" | custom-call | tf_op jit(solution)/shard_map/product/pallas_call | solution.py:239
  8.1 0.5 collective-permute-start
  8.6 0.1 collective-permute-start.1
  8.7 2.9 %collective-permute-start.2 = (f32[96,256]{1,0:T(8,128)S(1)}, f32[96,256]{1,0:T(8,128)S(1)}, u32[]{:S(2)}, u32[]{:S(2)}) collective-permute-start(f32[96,256]{1,0:T(8,128)S(1)} %get-tuple-element.25), channel_id=1, source_target_pairs={{0,2},{1,3},{2,0},{3,1},{4,6},{5,7},{6,4},{7,5},{8,10},{9,11},{10,... | collective-permute-start | bytes 294920 | tf_op jit(solution)/shard_map/ppermute | solution.py:339
  11.6 0.0 collective-permute-start.3
  11.6 0.0 collective-permute-done.1.refs_1_
  11.6 3.2 %collective-permute-done.2.refs_2_ = f32[96,256]{1,0:T(8,128)S(1)} collective-permute-done((f32[96,256]{1,0:T(8,128)S(1)}, f32[96,256]{1,0:T(8,128)S(1)}, u32[]{:S(2)}, u32[]{:S(2)}) %collective-permute-start.2) | collective-permute-done | bytes 98336 | tf_op jit(solution)/shard_map/ppermute | solution.py:339
  14.8 2.0 %collective-permute-done.3.refs_3_ = f32[96,256]{1,0:T(8,128)S(1)} collective-permute-done((f32[96,256]{1,0:T(8,128)S(1)}, f32[96,256]{1,0:T(8,128)S(1)}, u32[]{:S(2)}, u32[]{:S(2)}) %collective-permute-start.3) | collective-permute-done | bytes 98336 | tf_op jit(solution)/shard_map/ppermute | solution.py:339
  16.8 0.6 add_all.1.gate.own
  17.3 0.0 collective-permute-done.came
  17.3 0.6 add_and_part.1
  18.0 0.9 %collective-permute-start.4 = (f32[192,512]{1,0:T(8,128)S(1)}, f32[192,512]{1,0:T(8,128)S(1)}, u32[]{:S(2)}, u32[]{:S(2)}) collective-permute-start(f32[192,512]{1,0:T(8,128)S(1)} %get-tuple-element.28), channel_id=1, source_target_pairs={{0,2},{1,3},{2,0},{3,1},{4,6},{5,7},{6,4},{7,5},{8,10},{9,11},{10,... | collective-permute-start | bytes 1179656 | tf_op jit(solution)/shard_map/ppermute | solution.py:339
  18.9 2.5 %collective-permute-start.7 = (f32[96,256]{1,0:T(8,128)S(1)}, f32[96,256]{1,0:T(8,128)S(1)}, u32[]{:S(2)}, u32[]{:S(2)}) collective-permute-start(f32[96,256]{1,0:T(8,128)S(1)} %add_all.1.gate.own), channel_id=1, source_target_pairs={{0,12},{4,8},{8,4},{12,0},{16,28},{20,24},{24,20},{28,16},{1,13},{... | collective-permute-start | bytes 294920 | tf_op jit(solution)/shard_map/ppermute | solution.py:351
  21.4 0.4 collective-permute-start.6
  21.9 0.5 collective-permute-start.5
  22.4 3.0 %collective-permute-done.7.next_3 = f32[96,256]{1,0:T(8,128)S(1)} collective-permute-done((f32[96,256]{1,0:T(8,128)S(1)}, f32[96,256]{1,0:T(8,128)S(1)}, u32[]{:S(2)}, u32[]{:S(2)}) %collective-permute-start.7) | collective-permute-done | bytes 98336 | tf_op jit(solution)/shard_map/ppermute | solution.py:351
  25.4 1.7 %collective-permute-done.6.next_2 = f32[96,256]{1,0:T(8,128)S(1)} collective-permute-done((f32[96,256]{1,0:T(8,128)S(1)}, f32[96,256]{1,0:T(8,128)S(1)}, u32[]{:S(2)}, u32[]{:S(2)}) %collective-permute-start.6) | collective-permute-done | bytes 98336 | tf_op jit(solution)/shard_map/ppermute | solution.py:351
  27.1 0.0 collective-permute-done.5.next_1
  27.1 0.0 copy-done.1
  27.1 1.2 %two_levels.1 = (f32[96,512]{1,0:T(8,128)S(1)}, f32[96,256]{1,0:T(8,128)S(1)}, f32[96,256]{1,0:T(8,128)S(1)}, f32[96,256]{1,0:T(8,128)S(1)}) custom-call(s32[3]{0:T(128)S(1)} %pad_add_fusion.place.refs_0_, f32[96,256]{1,0:T(8,128)S(1)} %add_all.1.gate.own, f32[96,256]{1,0:T(8,128)S(1)} %collective-permute-done.5.next_1, ...), custom_call_target="tpu_custom_call" | custom-call | tf_op jit(solution)/shard_map/two_levels/pallas_call | solution.py:167
  28.3 0.8 %collective-permute-done.4.came = f32[192,512]{1,0:T(8,128)S(1)} collective-permute-done((f32[192,512]{1,0:T(8,128)S(1)}, f32[192,512]{1,0:T(8,128)S(1)}, u32[]{:S(2)}, u32[]{:S(2)}) %collective-permute-start.4) | collective-permute-done | bytes 393248 | tf_op jit(solution)/shard_map/ppermute | solution.py:339
  29.2 0.9 %leaf_kernel.1 = (f32[192,512]{1,0:T(8,128)S(1)}, f32[192,256]{1,0:T(8,128)S(1)}) custom-call(s32[3]{0:T(128)S(1)} %pad_add_fusion.place.refs_0_, f32[192,512]{1,0:T(8,128)S(1)} %get-tuple-element.27.held, f32[192,512]{1,0:T(8,128)S(1)} %collective-permute-done.4.came, s32[3,1,256]{2,1,0:T(1,128)S(1)} %bitcast.5, f32[96,512]{1,0:T(8,128)S(1)} %get-tuple-element.29.gate.node), custom_call_target="tpu_custom_call" | custom-call | tf_op jit(solution)/shard_map/leaf_kernel/pallas_call | solution.py:167
  30.1 0.1 collective-permute-start.11
  30.2 1.5 %collective-permute-start.12 = (f32[192,256]{1,0:T(8,128)S(1)}, f32[192,256]{1,0:T(8,128)S(1)}, u32[]{:S(2)}, u32[]{:S(2)}) collective-permute-start(f32[192,256]{1,0:T(8,128)S(1)} %get-tuple-element.35.own), channel_id=1, source_target_pairs={{0,2},{1,3},{2,0},{3,1},{4,6},{5,7},{6,4},{7,5},{8,10},{9,11},{10,... | collective-permute-start | bytes 589832 | tf_op jit(solution)/shard_map/ppermute | solution.py:339
  31.7 0.6 collective-permute-start.8
  32.2 3.5 %collective-permute-start.9 = (f32[96,256]{1,0:T(8,128)S(1)}, f32[96,256]{1,0:T(8,128)S(1)}, u32[]{:S(2)}, u32[]{:S(2)}) collective-permute-start(f32[96,256]{1,0:T(8,128)S(1)} %get-tuple-element.32), channel_id=1, source_target_pairs={{0,18},{1,19},{2,16},{3,17},{4,6},{5,7},{6,4},{7,5},{8,10},{9,11},... | collective-permute-start | bytes 294920 | tf_op jit(solution)/shard_map/ppermute | solution.py:377
  35.7 2.4 %collective-permute-start.10 = (f32[96,256]{1,0:T(8,128)S(1)}, f32[96,256]{1,0:T(8,128)S(1)}, u32[]{:S(2)}, u32[]{:S(2)}) collective-permute-start(f32[96,256]{1,0:T(8,128)S(1)} %get-tuple-element.33.top), channel_id=1, source_target_pairs={{0,16},{1,17},{2,18},{3,19},{16,0},{17,1},{18,2},{19,3}} | collective-permute-start | bytes 294920 | tf_op jit(solution)/shard_map/ppermute | solution.py:378
  38.2 1.9 %collective-permute-done.12.came = f32[192,256]{1,0:T(8,128)S(1)} collective-permute-done((f32[192,256]{1,0:T(8,128)S(1)}, f32[192,256]{1,0:T(8,128)S(1)}, u32[]{:S(2)}, u32[]{:S(2)}) %collective-permute-start.12) | collective-permute-done | bytes 196640 | tf_op jit(solution)/shard_map/ppermute | solution.py:339
  40.0 0.6 join_lanes.1.refs_3_
  40.6 0.1 collective-permute-start.13
  40.7 1.0 %collective-permute-done.8.first = f32[96,256]{1,0:T(8,128)S(1)} collective-permute-done((f32[96,256]{1,0:T(8,128)S(1)}, f32[96,256]{1,0:T(8,128)S(1)}, u32[]{:S(2)}, u32[]{:S(2)}) %collective-permute-start.8) | collective-permute-done | bytes 98336 | tf_op jit(solution)/shard_map/ppermute | solution.py:376
  41.7 0.0 collective-permute-done.9.second
  41.7 1.4 %collective-permute-done.10.third = f32[96,256]{1,0:T(8,128)S(1)} collective-permute-done((f32[96,256]{1,0:T(8,128)S(1)}, f32[96,256]{1,0:T(8,128)S(1)}, u32[]{:S(2)}, u32[]{:S(2)}) %collective-permute-start.10) | collective-permute-done | bytes 98336 | tf_op jit(solution)/shard_map/ppermute | solution.py:378
  43.1 0.0 collective-permute-done.11.refs_2_
  43.1 0.6 join_node.1.refs_5_
  43.7 0.1 collective-permute-start.14
  43.8 0.0 collective-permute-done.13.refs_4_
  43.8 1.7 %collective-permute-done.14.refs_6_ = f32[192,512]{1,0:T(8,128)S(1)} collective-permute-done((f32[192,512]{1,0:T(8,128)S(1)}, f32[192,512]{1,0:T(8,128)S(1)}, u32[]{:S(2)}, u32[]{:S(2)}) %collective-permute-start.14) | collective-permute-done | bytes 393248 | tf_op jit(solution)/shard_map/ppermute | solution.py:339
  45.5 23.1 %bases.1 = (f32[256,384]{1,0:T(8,128)}, f32[512,384]{1,0:T(8,128)}, f32[512,384]{1,0:T(8,128)}) custom-call(s32[3]{0:T(128)S(1)} %pad_add_fusion.place.refs_0_, f32[192,512]{1,0:T(8,128)S(1)} %get-tuple-element.30.refs_1_, f32[192,512]{1,0:T(8,128)S(1)} %collective-permute-done.11.refs_2_, f32[192,512]{1,0:T(8,128)S(1)} %join_lanes.1.refs_3_, ...), custom_call_target="tpu_custom_call" | custom-call | tf_op jit(solution)/shard_map/bases/pallas_call | solution.py:153
Async XLA Ops:
  0.6 26.5 %copy-start.1 = (s32[6,256]{1,0:T(8,128)S(1)}, s32[6,256]{1,0:T(8,128)}, u32[]{:S(2)}) copy-start(s32[6,256]{1,0:T(8,128)} %upper.1) | copy-start | bytes 18436
  0.7 0.7 copy-start
  8.1 9.2 %collective-permute-start = (f32[192,1024]{1,0:T(8,128)S(1)}, f32[192,1024]{1,0:T(8,128)S(1)}, u32[]{:S(2)}, u32[]{:S(2)}) collective-permute-start(f32[192,1024]{1,0:T(8,128)S(1)} %get-tuple-element.22), channel_id=1, source_target_pairs={{0,1},{1,0},{2,3},{3,2},{4,5},{5,4},{6,7},{7,6},{8,9},{9,8},{10,11... | collective-permute-start | bytes 2359304 | tf_op jit(solution)/shard_map/ppermute | solution.py:339
  8.6 3.0 %collective-permute-start.1 = (f32[96,256]{1,0:T(8,128)S(1)}, f32[96,256]{1,0:T(8,128)S(1)}, u32[]{:S(2)}, u32[]{:S(2)}) collective-permute-start(f32[96,256]{1,0:T(8,128)S(1)} %get-tuple-element.24), channel_id=1, source_target_pairs={{0,1},{1,0},{2,3},{3,2},{4,5},{5,4},{6,7},{7,6},{8,9},{9,8},{10,11... | collective-permute-start | bytes 294920 | tf_op jit(solution)/shard_map/ppermute | solution.py:339
  8.7 6.1 %collective-permute-start.2 = (f32[96,256]{1,0:T(8,128)S(1)}, f32[96,256]{1,0:T(8,128)S(1)}, u32[]{:S(2)}, u32[]{:S(2)}) collective-permute-start(f32[96,256]{1,0:T(8,128)S(1)} %get-tuple-element.25), channel_id=1, source_target_pairs={{0,2},{1,3},{2,0},{3,1},{4,6},{5,7},{6,4},{7,5},{8,10},{9,11},{10,... | collective-permute-start | bytes 294920 | tf_op jit(solution)/shard_map/ppermute | solution.py:339
  11.6 5.1 %collective-permute-start.3 = (f32[96,256]{1,0:T(8,128)S(1)}, f32[96,256]{1,0:T(8,128)S(1)}, u32[]{:S(2)}, u32[]{:S(2)}) collective-permute-start(f32[96,256]{1,0:T(8,128)S(1)} %get-tuple-element.26), channel_id=1, source_target_pairs={{0,3},{1,2},{2,1},{3,0},{4,7},{5,6},{6,5},{7,4},{8,11},{9,10},{10,... | collective-permute-start | bytes 294920 | tf_op jit(solution)/shard_map/ppermute | solution.py:339
  18.0 11.2 %collective-permute-start.4 = (f32[192,512]{1,0:T(8,128)S(1)}, f32[192,512]{1,0:T(8,128)S(1)}, u32[]{:S(2)}, u32[]{:S(2)}) collective-permute-start(f32[192,512]{1,0:T(8,128)S(1)} %get-tuple-element.28), channel_id=1, source_target_pairs={{0,2},{1,3},{2,0},{3,1},{4,6},{5,7},{6,4},{7,5},{8,10},{9,11},{10,... | collective-permute-start | bytes 1179656 | tf_op jit(solution)/shard_map/ppermute | solution.py:339
  18.9 6.5 %collective-permute-start.7 = (f32[96,256]{1,0:T(8,128)S(1)}, f32[96,256]{1,0:T(8,128)S(1)}, u32[]{:S(2)}, u32[]{:S(2)}) collective-permute-start(f32[96,256]{1,0:T(8,128)S(1)} %add_all.1.gate.own), channel_id=1, source_target_pairs={{0,12},{4,8},{8,4},{12,0},{16,28},{20,24},{24,20},{28,16},{1,13},{... | collective-permute-start | bytes 294920 | tf_op jit(solution)/shard_map/ppermute | solution.py:351
  21.4 5.7 %collective-permute-start.6 = (f32[96,256]{1,0:T(8,128)S(1)}, f32[96,256]{1,0:T(8,128)S(1)}, u32[]{:S(2)}, u32[]{:S(2)}) collective-permute-start(f32[96,256]{1,0:T(8,128)S(1)} %add_all.1.gate.own), channel_id=1, source_target_pairs={{0,8},{4,12},{8,0},{12,4},{16,24},{20,28},{24,16},{28,20},{1,9},{5... | collective-permute-start | bytes 294920 | tf_op jit(solution)/shard_map/ppermute | solution.py:351
  21.9 5.2 %collective-permute-start.5 = (f32[96,256]{1,0:T(8,128)S(1)}, f32[96,256]{1,0:T(8,128)S(1)}, u32[]{:S(2)}, u32[]{:S(2)}) collective-permute-start(f32[96,256]{1,0:T(8,128)S(1)} %add_all.1.gate.own), channel_id=1, source_target_pairs={{0,4},{4,0},{8,12},{12,8},{16,20},{20,16},{24,28},{28,24},{1,5},{5... | collective-permute-start | bytes 294920 | tf_op jit(solution)/shard_map/ppermute | solution.py:351
  30.1 13.1 %collective-permute-start.11 = (f32[192,512]{1,0:T(8,128)S(1)}, f32[192,512]{1,0:T(8,128)S(1)}, u32[]{:S(2)}, u32[]{:S(2)}) collective-permute-start(f32[192,512]{1,0:T(8,128)S(1)} %get-tuple-element.30.refs_1_), channel_id=1, source_target_pairs={{0,1},{1,0},{2,3},{3,2},{4,5},{5,4},{6,7},{7,6},{8,9},{9,8},{10,11... | collective-permute-start | bytes 1179656 | tf_op jit(solution)/shard_map/ppermute | solution.py:339
  30.2 9.9 %collective-permute-start.12 = (f32[192,256]{1,0:T(8,128)S(1)}, f32[192,256]{1,0:T(8,128)S(1)}, u32[]{:S(2)}, u32[]{:S(2)}) collective-permute-start(f32[192,256]{1,0:T(8,128)S(1)} %get-tuple-element.35.own), channel_id=1, source_target_pairs={{0,2},{1,3},{2,0},{3,1},{4,6},{5,7},{6,4},{7,5},{8,10},{9,11},{10,... | collective-permute-start | bytes 589832 | tf_op jit(solution)/shard_map/ppermute | solution.py:339
  31.7 10.0 %collective-permute-start.8 = (f32[96,256]{1,0:T(8,128)S(1)}, f32[96,256]{1,0:T(8,128)S(1)}, u32[]{:S(2)}, u32[]{:S(2)}) collective-permute-start(f32[96,256]{1,0:T(8,128)S(1)} %get-tuple-element.31), channel_id=1, source_target_pairs={{0,2},{1,3},{2,0},{3,1},{4,6},{5,7},{6,4},{7,5},{8,10},{9,11},{10,... | collective-permute-start | bytes 294920 | tf_op jit(solution)/shard_map/ppermute | solution.py:376
  32.2 9.4 %collective-permute-start.9 = (f32[96,256]{1,0:T(8,128)S(1)}, f32[96,256]{1,0:T(8,128)S(1)}, u32[]{:S(2)}, u32[]{:S(2)}) collective-permute-start(f32[96,256]{1,0:T(8,128)S(1)} %get-tuple-element.32), channel_id=1, source_target_pairs={{0,18},{1,19},{2,16},{3,17},{4,6},{5,7},{6,4},{7,5},{8,10},{9,11},... | collective-permute-start | bytes 294920 | tf_op jit(solution)/shard_map/ppermute | solution.py:377
  35.7 7.4 %collective-permute-start.10 = (f32[96,256]{1,0:T(8,128)S(1)}, f32[96,256]{1,0:T(8,128)S(1)}, u32[]{:S(2)}, u32[]{:S(2)}) collective-permute-start(f32[96,256]{1,0:T(8,128)S(1)} %get-tuple-element.33.top), channel_id=1, source_target_pairs={{0,16},{1,17},{2,18},{3,19},{16,0},{17,1},{18,2},{19,3}} | collective-permute-start | bytes 294920 | tf_op jit(solution)/shard_map/ppermute | solution.py:378
  40.6 3.2 %collective-permute-start.13 = (f32[192,512]{1,0:T(8,128)S(1)}, f32[192,512]{1,0:T(8,128)S(1)}, u32[]{:S(2)}, u32[]{:S(2)}) collective-permute-start(f32[192,512]{1,0:T(8,128)S(1)} %join_lanes.1.refs_3_), channel_id=1, source_target_pairs={{0,1},{1,0},{2,3},{3,2},{4,5},{5,4},{6,7},{7,6},{8,9},{9,8},{10,11... | collective-permute-start | bytes 1179656 | tf_op jit(solution)/shard_map/ppermute | solution.py:339
  43.7 1.8 %collective-permute-start.14 = (f32[192,512]{1,0:T(8,128)S(1)}, f32[192,512]{1,0:T(8,128)S(1)}, u32[]{:S(2)}, u32[]{:S(2)}) collective-permute-start(f32[192,512]{1,0:T(8,128)S(1)} %join_node.1.refs_5_), channel_id=1, source_target_pairs={{0,1},{1,0},{2,3},{3,2},{4,5},{5,4},{6,7},{7,6},{8,9},{9,8},{10,11... | collective-permute-start | bytes 1179656 | tf_op jit(solution)/shard_map/ppermute | solution.py:339

commit v3 on v1

--- a/solution.py
+++ b/solution.py
@@ -12,8 +12,8 @@
 BF16 = jnp.bfloat16
 PANEL = 128
 STRIP = 32
-AHEAD = 5
-PRODUCT_VMEM = 61 << 20
+AHEAD = 4
+PRODUCT_VMEM = 51 << 20
 SMALL_VMEM = 12 << 20
 BASES_VMEM = 24 << 20
 VMEM = pl.BlockSpec(memory_space=pltpu.VMEM)
@@ -47,42 +47,49 @@
     return jnp.broadcast_to(tile[:, lane : lane + 1], tile.shape)
 
 
-def eliminate(strips, first, width):
+def eliminate(strips, first, width, hold):
     tiles = STRIP // 8
     lane = lax.broadcasted_iota(jnp.int32, (8, width), 1)
     sub = lax.broadcasted_iota(jnp.int32, (8, width), 0)
     rows = [[strip[8 * t : 8 * t + 8] for t in range(tiles)] for strip in strips]
     pivots = [[None] * tiles for _ in strips]
-    columns = [
-        {k: {t: spread_lane(own[t], first + k) for t in range(tiles)} for k in range(AHEAD + 1)}
-        for own in rows
-    ]
+
+    def spread_from(own, k):
+        return {t: spread_lane(own[t], first + k) for t in range(k // 8, tiles)}
+
+    columns = [{k: spread_from(own, k) for k in range(AHEAD + 1)} for own in rows]
     for j in range(STRIP):
-        at, row = j // 8, j % 8
+        at, row, slot = j // 8, j % 8, j % hold.shape[1]
         below = sub > row
         here = lane == first + j
-        for own, ahead, seen in zip(rows, columns, pivots):
+        for m, (own, ahead, seen) in enumerate(zip(rows, columns, pivots)):
             column = ahead.pop(j)
             pivot = spread_row(column[at], row)
             seen[at] = pivot if row == 0 else jnp.where(sub >= row, pivot, seen[at])
             inverse = pl.reciprocal(pivot, approx=True)
+            for t in sorted({k // 8 for k in ahead if k > j + 1}):
+                hold[m, slot, t] = column[t]
+            hold[m, slot, tiles] = own[at]
             factor = {t: column[t] for t in range(at + 1, tiles)}
             if row < 7:
                 factor[at] = jnp.where(below, column[at], 0.0)
-            for later in ahead.values():
-                value = spread_row(later[at], row) * inverse
+            for k, later in ahead.items():
+                if k == j + 1:
+                    value = spread_row(column[k // 8], k % 8)
+                else:
+                    value = jnp.broadcast_to(hold[m, slot, k // 8, k % 8 : k % 8 + 1], (8, width))
+                value = value * inverse
                 for t in later:
                     if t in factor:
                         later[t] = later[t] - factor[t] * value
-            pivot_row = jnp.where(here, 1.0, spread_row(own[at], row)) * inverse
+            pivot_row = jnp.broadcast_to(hold[m, slot, tiles, row : row + 1], (8, width))
+            pivot_row = jnp.where(here, 1.0, pivot_row) * inverse
             for t in factor:
                 cleared = jnp.logical_and(here, below) if t == at else here
                 own[t] = jnp.where(cleared, 0.0, own[t]) - factor[t] * pivot_row
             new = j + AHEAD + 1
             if new < STRIP:
-                ahead[new] = {
-                    t: spread_lane(own[t], first + new) for t in range((j + 1) // 8, tiles)
-                }
+                ahead[new] = spread_from(own, new)
     scaled = []
     for own, seen in zip(rows, pivots):
         out = []
@@ -95,13 +102,13 @@
     return scaled
 
 
-def panel_inverses(panels):
+def panel_inverses(panels, hold):
     width = panels[0].shape[0]
     rest = list(panels)
     inverse_rows = [[] for _ in panels]
     for first in range(0, width, STRIP):
         past = first + STRIP
-        strips = eliminate([one[:STRIP] for one in rest], first, width)
+        strips = eliminate([one[:STRIP] for one in rest], first, width, hold)
         lane = lax.broadcasted_iota(jnp.int32, (STRIP, width), 1)
         for m, strip in enumerate(strips):
             inverse_rows[m].append(jnp.where(lane < past, strip, 0.0))
@@ -115,15 +122,16 @@
 
 
 def basis_kernel(*refs, count, bits):
-    place, parts, bases = refs[0], refs[1 : 1 + 2 * count], refs[1 + 2 * count : 1 + 3 * count]
-    held, grams = refs[1 + 3 * count : 1 + 4 * count], refs[1 + 4 * count : 1 + 5 * count]
-    leaf = refs[1 + 5 * count]
+    place, own, came, *refs = refs
+    bases, held, grams = refs[:count], refs[count : 2 * count], refs[2 * count : 3 * count]
+    leaf, hold = refs[3 * count :]
     columns, rows = held[0].shape
     scale = math.sqrt(rows)
     half = columns // 2
     for m, source in enumerate(held):
-        source[pl.ds(pl.multiple_of(place[0] * half, half), half), :] = parts[2 * m][...]
-        source[pl.ds(pl.multiple_of(half - place[0] * half, half), half), :] = parts[2 * m + 1][...]
+        lanes = slice(m * rows, m * rows + rows)
+        source[pl.ds(pl.multiple_of(place[0] * half, half), half), :] = own[:, lanes]
+        source[pl.ds(pl.multiple_of(half - place[0] * half, half), half), :] = came[:, lanes]
     for source, gram in zip(held, grams):
         value = source[...]
         gram[...] = dot3(value, value, 1, 1)
@@ -134,7 +142,7 @@
     for start in range(0, columns, PANEL):
         own, after = slice(start, start + PANEL), slice(start + PANEL, columns)
         last = start + PANEL == columns
-        inverses = panel_inverses([gram[own, own] for gram in grams])
+        inverses = panel_inverses([gram[own, own] for gram in grams], hold)
         for inverse, source, gram, basis in zip(inverses, held, grams, bases):
             if not last:
                 lower = dot3(gram[after, own], inverse, 1, 1)
@@ -145,22 +153,22 @@
                 source[after, :] = source[after, :] - dot3(lower, block, 1, 0)
 
 
-def bases_of(place, parts, share):
-    count = len(parts) // 2
-    columns, rows = 2 * parts[0].shape[0], parts[0].shape[1]
+def bases_of(place, own, came, share):
+    count = 3
+    columns, rows = 2 * own.shape[0], own.shape[1] // count
     bits = lax.axis_size("samples").bit_length() - 1
     shapes = [(share if m == 0 else rows, columns) for m in range(count)]
     return pl.pallas_call(
         functools.partial(basis_kernel, count=count, bits=bits),
         out_shape=[jax.ShapeDtypeStruct(shape, F32) for shape in shapes],
-        in_specs=[SMEM] + [VMEM] * len(parts),
+        in_specs=[SMEM, VMEM, VMEM],
         out_specs=[VMEM] * count,
         scratch_shapes=[pltpu.VMEM((columns, rows), F32)] * count
         + [pltpu.VMEM((columns, columns), F32)] * count
-        + [pltpu.VMEM((columns, share), F32)],
+        + [pltpu.VMEM((columns, share), F32), pltpu.VMEM((count, 4, STRIP // 8 + 1, 8, PANEL), F32)],
         compiler_params=pltpu.CompilerParams(vmem_limit_bytes=BASES_VMEM),
         name="bases",
-    )(place, *parts)
+    )(place, own, came)
 
 
 def call(kernel, shapes, *operands, **static):
@@ -260,25 +268,21 @@
     other[...] = part(held, 1 - place[bit], half) + part(came, 1 - place[bit], half)
 
 
-def add_and_part(place, held, came, own, other, *, bit):
+def add_and_part(place, held, came, pivots, gate, own, kept, sent, *, bit):
     leaf = own.shape[1]
-    for index, out in ((place[bit], own), (1 - place[bit], other)):
+    parts = []
+    for index in (place[bit], 1 - place[bit]):
         lanes = pl.ds(pl.multiple_of(index * leaf, leaf), leaf)
-        out[...] = held[:, lanes] + came[:, lanes]
+        parts.append(held[:, lanes] + came[:, lanes])
+    mine, theirs = parts
+    own[...] = mine
+    kept[...] = pick(theirs, pivots[1 - place[bit]])
+    sent[:, :leaf] = theirs
+    sent[:, leaf:] = pick(mine, pivots[place[bit]])
 
 
 def add_all(place, *refs):
     refs[-1][...] = sum(ref[...] for ref in refs[1:-1]) + refs[0][...]
-
-
-def leaf_kernel(place, held, came, pivots, leaf, skeleton, *, bit):
-    value = held[...] + came[...]
-    leaf[...] = value
-    skeleton[...] = pick(value, pivots[place[bit]])
-
-
-def join_lanes(place, own, came, out, *, bit):
-    out[...] = ordered(own[...], came[...], place[bit] == 1)
 
 
 def join_rows(place, own, came, out, *, bit):
@@ -323,15 +327,23 @@
     messages(position, chosen, raised, first, second, count)
 
 
-def join_node(place, node, top, first, second, third, out, *, at, count, bit):
+def join_all(
+    place, node, top, first, second, third, own, kept, came, pivots, out, *, at, count, bit
+):
+    leaf, rank = own.shape[1], kept.shape[1]
+    value = own[...] + came[:, :leaf]
+    out[:, :leaf] = value
+    skeleton = pick(value, pivots[place[bit]])
+    other = kept[...] + came[:, leaf:]
+    out[:, leaf : leaf + 2 * rank] = ordered(skeleton, other, place[bit] == 1)
     root = place[at] % (count // 2) == 0
     right = place[at] == count // 2
     own_root = ordered(top[...], third[...], right)
     half = node.shape[0]
     mine = pl.ds(pl.multiple_of(place[bit] * half, half), half)
     theirs = pl.ds(pl.multiple_of(half - place[bit] * half, half), half)
-    out[mine, :] = jnp.where(root, own_root, node[...])
-    out[theirs, :] = ordered(first[...], second[...], right)
+    out[mine, leaf + 2 * rank :] = jnp.where(root, own_root, node[...])
+    out[theirs, leaf + 2 * rank :] = ordered(first[...], second[...], right)
 
 
 def exchange(block, other):
@@ -376,10 +388,7 @@
     first = lax.ppermute(first, axes, across)
     second = lax.ppermute(second, axes, other_side)
     third = lax.ppermute(top, axes, along)
-    half = (2 * wide[0], wide[1])
-    return call(
-        join_node, [half], place, node, top, first, second, third, at=at, count=count, bit=bit
-    )[0]
+    return node, top, first, second, third
 
 
 def on_device(matrix_block, sketch_matrix, local_pivots, upper_pivots):
@@ -393,34 +402,32 @@
     own, other, *tops = product(place, matrix_block, sketch_matrix, pivots, bits)
     tops = tops[:1] + [exchange(top, x) for x, top in enumerate(tops) if x > 0]
     came = exchange(other, 1)
-    own, came, tops = lax.optimization_barrier((own, came, tops))
     for bit in range(1, bits - 1):
         half = (own.shape[0] // 2, rows)
         own, other = call(add_and_halve, [half] * 2, place, own, came, bit=bit)
         came = swap(other, bit)
+    top = call(add_all, [tops[0].shape], place, *tops)[0]
     last = bits - 1
     leaf_shape = (own.shape[0], rows // 2)
-    own, other = call(add_and_part, [leaf_shape] * 2, place, own, came, bit=last)
-    came = swap(other, last)
-
-    top = call(add_all, [tops[0].shape], place, *tops)[0]
-    node = climb(place, top, upper_pivots, bits, bits)
-
-    leaf, skeleton = call(
-        leaf_kernel, [leaf_shape, (leaf_shape[0], rank)], place, own, came, pivots, bit=last
+    sent_shape = (leaf_shape[0], leaf_shape[1] + rank)
+    own, kept, sent = call(
+        add_and_part,
+        [leaf_shape, (leaf_shape[0], rank), sent_shape],
+        place, own, came, pivots, top, bit=last,
     )
-    skeleton_came = swap(skeleton, last)
-    stacked = call(
-        join_lanes, [(leaf_shape[0], 2 * rank)], place, skeleton, skeleton_came, bit=last
+    came = swap(sent, last)
+    node, top, *arrived = climb(place, top, upper_pivots, bits, bits)
+    *arrived, came = lax.optimization_barrier((*arrived, came))
+    held = call(
+        join_all,
+        [(leaf_shape[0], leaf_shape[1] + 4 * rank)],
+        place, node, top, *arrived, own, kept, came, pivots, at=bits,
+        count=lax.axis_size("rows"), bit=last,
     )[0]
-    held = [leaf, stacked, node]
     for bit in range(bits - 2, 0, -1):
-        whole = (2 * held[0].shape[0], held[0].shape[1])
-        held = [call(join_rows, [whole], place, one, swap(one, bit), bit=bit)[0] for one in held]
-    parts = []
-    for one in held:
-        parts += [one, swap(one, 0)]
-    return tuple(bases_of(place, parts, rows // shares))
+        whole = (2 * held.shape[0], held.shape[1])
+        held = call(join_rows, [whole], place, held, swap(held, bit), bit=bit)[0]
+    return tuple(bases_of(place, held, exchange(held, 1), rows // shares))
 
 
 def solution(mesh):

time: 72.8 us -> 63.3 us (0.87)
  Pallas kernels: 35.2 us -> 29.4 us
  starting transfers between devices: 16.8 us -> 14.5 us
  local copies, waits for them, and re-layouts: 2.04 us -> 0.69 us
    ppermute x3, waiting for transfers between devices: 0.01 us -> 4.71 us  [climb(): lax.ppermute(current, 'rows', [(d, d ^ step) for d in range(count)])]
    pallas_call x1, Pallas kernels: 23.1 us -> 18.9 us  [bases_of(): pl.pallas_call(functools.partial(basis_kernel, count=count, bits=bits), o...]
    ppermute x9 -> x6, waiting for transfers between devices: 12.2 us -> 7.98 us  [exchange(): lax.ppermute(block, 'samples', [(s, s ^ other) for s in range(count)])]
    ppermute x9 -> x6, starting transfers between devices: 6.69 us -> 4.52 us  [exchange(): lax.ppermute(block, 'samples', [(s, s ^ other) for s in range(count)])]
    ppermute x1, waiting for transfers between devices: 3.63 us -> 2.26 us  [climb(): third = lax.ppermute(top, axes, along)]
    ppermute x1, waiting for transfers between devices: 1.35 us -> 2.72 us  [climb(): first = lax.ppermute(first, axes, across)]
    unnamed x10 -> x4, local copies, waits for them, and re-layouts: 2.04 us -> 0.69 us
    pallas_call x1, Pallas kernels: 7.6 us -> 6.68 us  [product(): pl.pallas_call(functools.partial(product_kernel, bits=bits), out_shape=[j...]
  transfers between devices with their start and end apart: 15 -> 12, of which waited for: 8 -> 7; matrix products, arithmetic and copies ran while one was open for 0% -> 0% of each run, Pallas kernels for 5% -> 3%
where the time goes in v3:
time: 63.3 us; the launch traced here: 63.1 us
  Pallas kernels  29.4 us (46%)
  waiting for transfers between devices  17.7 us (28%)
  starting transfers between devices  14.5 us (23%)
  between operations  0.71 us (1%)
  local copies, waits for them, and re-layouts  0.69 us (1%)
    pallas_call x1, Pallas kernels, bases_of(): pl.pallas_call(functools.partial(basis_kernel, count=count, bits=bits), o...  18.9 us
    ppermute x6, waiting for transfers between devices, exchange(): lax.ppermute(block, 'samples', [(s, s ^ other) for s in range(count)])  7.98 us
    pallas_call x1, Pallas kernels, product(): pl.pallas_call(functools.partial(product_kernel, bits=bits), out_shape=[j...  6.68 us
    ppermute x3, waiting for transfers between devices, climb(): lax.ppermute(current, 'rows', [(d, d ^ step) for d in range(count)])  4.71 us
    ppermute x6, starting transfers between devices, exchange(): lax.ppermute(block, 'samples', [(s, s ^ other) for s in range(count)])  4.52 us
    pallas_call x4, Pallas kernels, call(): pl.pallas_call(functools.partial(kernel, **static), out_shape=[jax.ShapeD...  3.83 us
    ppermute x3, starting transfers between devices, climb(): lax.ppermute(current, 'rows', [(d, d ^ step) for d in range(count)])  3.49 us
    ppermute x1, starting transfers between devices, climb(): second = lax.ppermute(second, axes, other_side)  3.36 us
  transfers between devices with their start and end apart: 12, of which 7 were waited for; matrix products, arithmetic and copies ran while one was open for 0% of the time, Pallas kernels for 3%

profile of v3, /device:TPU:0, one launch (start us, length us, event | category | flops | bytes accessed | tf_op | source)
XLA Modules:
  0.0 63.1 jit_solution(12001780601125965139)
XLA Ops:
  0.6 0.1 pad_add_fusion.place.refs_0_
  0.7 0.0 copy-start
  0.7 0.7 %copy-done = s32[1,3,256]{2,0,1:T(1,128)S(1)} copy-done((s32[1,3,256]{2,0,1:T(1,128)S(1)}, s32[1,3,256]{2,0,1:T(1,128)}, u32[]{:S(2)}) %copy-start) | copy-done | bytes 3096
  1.4 6.7 %product.1 = (f32[192,1024]{1,0:T(8,128)S(1)}, f32[192,1024]{1,0:T(8,128)S(1)}, f32[96,256]{1,0:T(8,128)S(1)}, f32[96,256]{1,0:T(8,128)S(1)}, f32[96,256]{1,0:T(8,128)S(1)}, /*index=5*/f32[96,256]{1,0:T(8,128)S(1)}) custom-call(s32[3]{0:T(128)S(1)} %pad_add_fusion.place.refs_0_, bf16[1024,2560]{1,0:T(8,128)(2,1)} %matrix.1, bf16[2560,384]{1,0:T(8,128)(2,1)} %sketch.1, ...), custom_call_target="tpu_custom_call" | custom-call | tf_op jit(solution)/shard_map/product/pallas_call | solution.py:247
  8.1 0.0 copy-start.1
  8.1 0.5 collective-permute-start.9
  8.6 0.1 collective-permute-start
  8.7 2.9 %collective-permute-start.1 = (f32[96,256]{1,0:T(8,128)S(1)}, f32[96,256]{1,0:T(8,128)S(1)}, u32[]{:S(2)}, u32[]{:S(2)}) collective-permute-start(f32[96,256]{1,0:T(8,128)S(1)} %get-tuple-element.22), channel_id=1, source_target_pairs={{0,2},{1,3},{2,0},{3,1},{4,6},{5,7},{6,4},{7,5},{8,10},{9,11},{10,... | collective-permute-start | bytes 294920 | tf_op jit(solution)/shard_map/ppermute | solution.py:351
  11.6 0.0 collective-permute-start.2
  11.6 0.0 collective-permute-done.refs_1_
  11.6 3.2 %collective-permute-done.1.refs_2_ = f32[96,256]{1,0:T(8,128)S(1)} collective-permute-done((f32[96,256]{1,0:T(8,128)S(1)}, f32[96,256]{1,0:T(8,128)S(1)}, u32[]{:S(2)}, u32[]{:S(2)}) %collective-permute-start.1) | collective-permute-done | bytes 98336 | tf_op jit(solution)/shard_map/ppermute | solution.py:351
  14.8 2.0 %collective-permute-done.2.refs_3_ = f32[96,256]{1,0:T(8,128)S(1)} collective-permute-done((f32[96,256]{1,0:T(8,128)S(1)}, f32[96,256]{1,0:T(8,128)S(1)}, u32[]{:S(2)}, u32[]{:S(2)}) %collective-permute-start.2) | collective-permute-done | bytes 98336 | tf_op jit(solution)/shard_map/ppermute | solution.py:351
  16.8 0.6 add_all.1.own.gate
  17.3 0.0 collective-permute-done.9.came
  17.3 1.1 %add_and_part.1 = (f32[192,512]{1,0:T(8,128)S(1)}, f32[192,256]{1,0:T(8,128)S(1)}, f32[192,768]{1,0:T(8,128)S(1)}) custom-call(s32[3]{0:T(128)S(1)} %pad_add_fusion.place.refs_0_, f32[192,1024]{1,0:T(8,128)S(1)} %get-tuple-element.28.held, f32[192,1024]{1,0:T(8,128)S(1)} %collective-permute-done.9.came, s32[3,1,256]{2,1,0:T(1,128)S(1)} %bitcast.5, ...), custom_call_target="tpu_custom_call" | custom-call | tf_op jit(solution)/shard_map/add_and_part/pallas_call | solution.py:175
  18.4 0.9 %collective-permute-start.10 = (f32[192,768]{1,0:T(8,128)S(1)}, f32[192,768]{1,0:T(8,128)S(1)}, u32[]{:S(2)}, u32[]{:S(2)}) collective-permute-start(f32[192,768]{1,0:T(8,128)S(1)} %get-tuple-element.30), channel_id=1, source_target_pairs={{0,2},{1,3},{2,0},{3,1},{4,6},{5,7},{6,4},{7,5},{8,10},{9,11},{10,... | collective-permute-start | bytes 1769480 | tf_op jit(solution)/shard_map/ppermute | solution.py:351
  19.4 2.5 %collective-permute-start.5 = (f32[96,256]{1,0:T(8,128)S(1)}, f32[96,256]{1,0:T(8,128)S(1)}, u32[]{:S(2)}, u32[]{:S(2)}) collective-permute-start(f32[96,256]{1,0:T(8,128)S(1)} %add_all.1.own.gate), channel_id=1, source_target_pairs={{0,12},{4,8},{8,4},{12,0},{16,28},{20,24},{24,20},{28,16},{1,13},{... | collective-permute-start | bytes 294920 | tf_op jit(solution)/shard_map/ppermute | solution.py:363
  21.9 0.5 collective-permute-start.4
  22.4 0.5 collective-permute-start.3
  22.9 3.0 %collective-permute-done.5.next_3 = f32[96,256]{1,0:T(8,128)S(1)} collective-permute-done((f32[96,256]{1,0:T(8,128)S(1)}, f32[96,256]{1,0:T(8,128)S(1)}, u32[]{:S(2)}, u32[]{:S(2)}) %collective-permute-start.5) | collective-permute-done | bytes 98336 | tf_op jit(solution)/shard_map/ppermute | solution.py:363
  25.9 1.7 %collective-permute-done.4.next_2 = f32[96,256]{1,0:T(8,128)S(1)} collective-permute-done((f32[96,256]{1,0:T(8,128)S(1)}, f32[96,256]{1,0:T(8,128)S(1)}, u32[]{:S(2)}, u32[]{:S(2)}) %collective-permute-start.4) | collective-permute-done | bytes 98336 | tf_op jit(solution)/shard_map/ppermute | solution.py:363
  27.6 0.0 collective-permute-done.3.next_1
  27.6 0.0 copy-done.1
  27.6 1.2 %two_levels.1 = (f32[96,512]{1,0:T(8,128)S(1)}, f32[96,256]{1,0:T(8,128)S(1)}, f32[96,256]{1,0:T(8,128)S(1)}, f32[96,256]{1,0:T(8,128)S(1)}) custom-call(s32[3]{0:T(128)S(1)} %pad_add_fusion.place.refs_0_, f32[96,256]{1,0:T(8,128)S(1)} %add_all.1.own.gate, f32[96,256]{1,0:T(8,128)S(1)} %collective-permute-done.3.next_1, ...), custom_call_target="tpu_custom_call" | custom-call | tf_op jit(solution)/shard_map/two_levels/pallas_call | solution.py:175
  28.8 0.8 %collective-permute-start.6 = (f32[96,256]{1,0:T(8,128)S(1)}, f32[96,256]{1,0:T(8,128)S(1)}, u32[]{:S(2)}, u32[]{:S(2)}) collective-permute-start(f32[96,256]{1,0:T(8,128)S(1)} %get-tuple-element.26), channel_id=1, source_target_pairs={{0,2},{1,3},{2,0},{3,1},{4,6},{5,7},{6,4},{7,5},{8,10},{9,11},{10,... | collective-permute-start | bytes 294920 | tf_op jit(solution)/shard_map/ppermute | solution.py:388
  29.5 3.4 %collective-permute-start.7 = (f32[96,256]{1,0:T(8,128)S(1)}, f32[96,256]{1,0:T(8,128)S(1)}, u32[]{:S(2)}, u32[]{:S(2)}) collective-permute-start(f32[96,256]{1,0:T(8,128)S(1)} %get-tuple-element.27), channel_id=1, source_target_pairs={{0,18},{1,19},{2,16},{3,17},{4,6},{5,7},{6,4},{7,5},{8,10},{9,11},... | collective-permute-start | bytes 294920 | tf_op jit(solution)/shard_map/ppermute | solution.py:389
  32.9 2.4 %collective-permute-start.8 = (f32[96,256]{1,0:T(8,128)S(1)}, f32[96,256]{1,0:T(8,128)S(1)}, u32[]{:S(2)}, u32[]{:S(2)}) collective-permute-start(f32[96,256]{1,0:T(8,128)S(1)} %get-tuple-element.25.top), channel_id=1, source_target_pairs={{0,16},{1,17},{2,18},{3,19},{16,0},{17,1},{18,2},{19,3}} | collective-permute-start | bytes 294920 | tf_op jit(solution)/shard_map/ppermute | solution.py:390
  35.3 2.7 %collective-permute-done.6.first = f32[96,256]{1,0:T(8,128)S(1)} collective-permute-done((f32[96,256]{1,0:T(8,128)S(1)}, f32[96,256]{1,0:T(8,128)S(1)}, u32[]{:S(2)}, u32[]{:S(2)}) %collective-permute-start.6) | collective-permute-done | bytes 98336 | tf_op jit(solution)/shard_map/ppermute | solution.py:388
  38.1 0.0 collective-permute-done.7.second
  38.1 2.3 %collective-permute-done.8.third = f32[96,256]{1,0:T(8,128)S(1)} collective-permute-done((f32[96,256]{1,0:T(8,128)S(1)}, f32[96,256]{1,0:T(8,128)S(1)}, u32[]{:S(2)}, u32[]{:S(2)}) %collective-permute-start.8) | collective-permute-done | bytes 98336 | tf_op jit(solution)/shard_map/ppermute | solution.py:390
  40.3 0.0 collective-permute-done.10.came
  40.3 1.0 %join_all.1.refs_1_ = f32[192,1536]{1,0:T(8,128)S(1)} custom-call(s32[3]{0:T(128)S(1)} %pad_add_fusion.place.refs_0_, f32[96,512]{1,0:T(8,128)S(1)} %get-tuple-element.24.node, f32[96,256]{1,0:T(8,128)S(1)} %get-tuple-element.25.top, f32[96,256]{1,0:T(8,128)S(1)} %collective-permute-done.6.first, f32[96,256]{1,0:T(8,128)S(1)} %collective-permute-done.7.second, ...), custom_call_target="tpu_custom_call" | custom-call | tf_op jit(solution)/shard_map/join_all/pallas_call | solution.py:175
  41.3 0.1 collective-permute-start.11
  41.4 2.8 %collective-permute-done.11.refs_2_ = f32[192,1536]{1,0:T(8,128)S(1)} collective-permute-done((f32[192,1536]{1,0:T(8,128)S(1)}, f32[192,1536]{1,0:T(8,128)S(1)}, u32[]{:S(2)}, u32[]{:S(2)}) %collective-permute-start.11) | collective-permute-done | bytes 1179680 | tf_op jit(solution)/shard_map/ppermute | solution.py:351
  44.2 18.9 %bases.1 = (f32[256,384]{1,0:T(8,128)}, f32[512,384]{1,0:T(8,128)}, f32[512,384]{1,0:T(8,128)}) custom-call(s32[3]{0:T(128)S(1)} %pad_add_fusion.place.refs_0_, f32[192,1536]{1,0:T(8,128)S(1)} %join_all.1.refs_1_, f32[192,1536]{1,0:T(8,128)S(1)} %collective-permute-done.11.refs_2_), custom_call_target="tpu_custom_call" | custom-call | tf_op jit(solution)/shard_map/bases/pallas_call | solution.py:161
Async XLA Ops:
  0.7 0.7 %copy-start = (s32[1,3,256]{2,0,1:T(1,128)S(1)}, s32[1,3,256]{2,0,1:T(1,128)}, u32[]{:S(2)}) copy-start(s32[1,3,256]{2,0,1:T(1,128)} %param.6) | copy-start | bytes 9220
  8.1 19.5 %copy-start.1 = (s32[6,256]{1,0:T(8,128)S(1)}, s32[6,256]{1,0:T(8,128)}, u32[]{:S(2)}) copy-start(s32[6,256]{1,0:T(8,128)} %upper.1) | copy-start | bytes 18436
  8.1 9.2 %collective-permute-start.9 = (f32[192,1024]{1,0:T(8,128)S(1)}, f32[192,1024]{1,0:T(8,128)S(1)}, u32[]{:S(2)}, u32[]{:S(2)}) collective-permute-start(f32[192,1024]{1,0:T(8,128)S(1)} %get-tuple-element.29), channel_id=1, source_target_pairs={{0,1},{1,0},{2,3},{3,2},{4,5},{5,4},{6,7},{7,6},{8,9},{9,8},{10,11... | collective-permute-start | bytes 2359304 | tf_op jit(solution)/shard_map/ppermute | solution.py:351
  8.6 3.0 %collective-permute-start = (f32[96,256]{1,0:T(8,128)S(1)}, f32[96,256]{1,0:T(8,128)S(1)}, u32[]{:S(2)}, u32[]{:S(2)}) collective-permute-start(f32[96,256]{1,0:T(8,128)S(1)} %get-tuple-element.21), channel_id=1, source_target_pairs={{0,1},{1,0},{2,3},{3,2},{4,5},{5,4},{6,7},{7,6},{8,9},{9,8},{10,11... | collective-permute-start | bytes 294920 | tf_op jit(solution)/shard_map/ppermute | solution.py:351
  8.7 6.1 %collective-permute-start.1 = (f32[96,256]{1,0:T(8,128)S(1)}, f32[96,256]{1,0:T(8,128)S(1)}, u32[]{:S(2)}, u32[]{:S(2)}) collective-permute-start(f32[96,256]{1,0:T(8,128)S(1)} %get-tuple-element.22), channel_id=1, source_target_pairs={{0,2},{1,3},{2,0},{3,1},{4,6},{5,7},{6,4},{7,5},{8,10},{9,11},{10,... | collective-permute-start | bytes 294920 | tf_op jit(solution)/shard_map/ppermute | solution.py:351
  11.6 5.1 %collective-permute-start.2 = (f32[96,256]{1,0:T(8,128)S(1)}, f32[96,256]{1,0:T(8,128)S(1)}, u32[]{:S(2)}, u32[]{:S(2)}) collective-permute-start(f32[96,256]{1,0:T(8,128)S(1)} %get-tuple-element.23), channel_id=1, source_target_pairs={{0,3},{1,2},{2,1},{3,0},{4,7},{5,6},{6,5},{7,4},{8,11},{9,10},{10,... | collective-permute-start | bytes 294920 | tf_op jit(solution)/shard_map/ppermute | solution.py:351
  18.4 21.9 %collective-permute-start.10 = (f32[192,768]{1,0:T(8,128)S(1)}, f32[192,768]{1,0:T(8,128)S(1)}, u32[]{:S(2)}, u32[]{:S(2)}) collective-permute-start(f32[192,768]{1,0:T(8,128)S(1)} %get-tuple-element.30), channel_id=1, source_target_pairs={{0,2},{1,3},{2,0},{3,1},{4,6},{5,7},{6,4},{7,5},{8,10},{9,11},{10,... | collective-permute-start | bytes 1769480 | tf_op jit(solution)/shard_map/ppermute | solution.py:351
  19.4 6.5 %collective-permute-start.5 = (f32[96,256]{1,0:T(8,128)S(1)}, f32[96,256]{1,0:T(8,128)S(1)}, u32[]{:S(2)}, u32[]{:S(2)}) collective-permute-start(f32[96,256]{1,0:T(8,128)S(1)} %add_all.1.own.gate), channel_id=1, source_target_pairs={{0,12},{4,8},{8,4},{12,0},{16,28},{20,24},{24,20},{28,16},{1,13},{... | collective-permute-start | bytes 294920 | tf_op jit(solution)/shard_map/ppermute | solution.py:363
  21.9 5.7 %collective-permute-start.4 = (f32[96,256]{1,0:T(8,128)S(1)}, f32[96,256]{1,0:T(8,128)S(1)}, u32[]{:S(2)}, u32[]{:S(2)}) collective-permute-start(f32[96,256]{1,0:T(8,128)S(1)} %add_all.1.own.gate), channel_id=1, source_target_pairs={{0,8},{4,12},{8,0},{12,4},{16,24},{20,28},{24,16},{28,20},{1,9},{5... | collective-permute-start | bytes 294920 | tf_op jit(solution)/shard_map/ppermute | solution.py:363
  22.4 5.2 %collective-permute-start.3 = (f32[96,256]{1,0:T(8,128)S(1)}, f32[96,256]{1,0:T(8,128)S(1)}, u32[]{:S(2)}, u32[]{:S(2)}) collective-permute-start(f32[96,256]{1,0:T(8,128)S(1)} %add_all.1.own.gate), channel_id=1, source_target_pairs={{0,4},{4,0},{8,12},{12,8},{16,20},{20,16},{24,28},{28,24},{1,5},{5... | collective-permute-start | bytes 294920 | tf_op jit(solution)/shard_map/ppermute | solution.py:363
  28.8 9.3 %collective-permute-start.6 = (f32[96,256]{1,0:T(8,128)S(1)}, f32[96,256]{1,0:T(8,128)S(1)}, u32[]{:S(2)}, u32[]{:S(2)}) collective-permute-start(f32[96,256]{1,0:T(8,128)S(1)} %get-tuple-element.26), channel_id=1, source_target_pairs={{0,2},{1,3},{2,0},{3,1},{4,6},{5,7},{6,4},{7,5},{8,10},{9,11},{10,... | collective-permute-start | bytes 294920 | tf_op jit(solution)/shard_map/ppermute | solution.py:388
  29.5 8.5 %collective-permute-start.7 = (f32[96,256]{1,0:T(8,128)S(1)}, f32[96,256]{1,0:T(8,128)S(1)}, u32[]{:S(2)}, u32[]{:S(2)}) collective-permute-start(f32[96,256]{1,0:T(8,128)S(1)} %get-tuple-element.27), channel_id=1, source_target_pairs={{0,18},{1,19},{2,16},{3,17},{4,6},{5,7},{6,4},{7,5},{8,10},{9,11},... | collective-permute-start | bytes 294920 | tf_op jit(solution)/shard_map/ppermute | solution.py:389
  32.9 7.4 %collective-permute-start.8 = (f32[96,256]{1,0:T(8,128)S(1)}, f32[96,256]{1,0:T(8,128)S(1)}, u32[]{:S(2)}, u32[]{:S(2)}) collective-permute-start(f32[96,256]{1,0:T(8,128)S(1)} %get-tuple-element.25.top), channel_id=1, source_target_pairs={{0,16},{1,17},{2,18},{3,19},{16,0},{17,1},{18,2},{19,3}} | collective-permute-start | bytes 294920 | tf_op jit(solution)/shard_map/ppermute | solution.py:390
  41.3 2.9 %collective-permute-start.11 = (f32[192,1536]{1,0:T(8,128)S(1)}, f32[192,1536]{1,0:T(8,128)S(1)}, u32[]{:S(2)}, u32[]{:S(2)}) collective-permute-start(f32[192,1536]{1,0:T(8,128)S(1)} %join_all.1.refs_1_), channel_id=1, source_target_pairs={{0,1},{1,0},{2,3},{3,2},{4,5},{5,4},{6,7},{7,6},{8,9},{9,8},{10,11... | collective-permute-start | bytes 3538952 | tf_op jit(solution)/shard_map/ppermute | solution.py:351

commit v4 on v3

--- a/solution.py
+++ b/solution.py
@@ -124,7 +124,8 @@
 def basis_kernel(*refs, count, bits):
     place, own, came, *refs = refs
     bases, held, grams = refs[:count], refs[count : 2 * count], refs[2 * count : 3 * count]
-    leaf, hold = refs[3 * count :]
+    leaf, hold, *made, sems = refs[3 * count :]
+    copies = []
     columns, rows = held[0].shape
     scale = math.sqrt(rows)
     half = columns // 2
@@ -133,8 +134,9 @@
         source[pl.ds(pl.multiple_of(place[0] * half, half), half), :] = own[:, lanes]
         source[pl.ds(pl.multiple_of(half - place[0] * half, half), half), :] = came[:, lanes]
     for source, gram in zip(held, grams):
-        value = source[...]
-        gram[...] = dot3(value, value, 1, 1)
+        for start in range(0, columns, PANEL):
+            own_rows = slice(start, start + PANEL)
+            gram[start:, own_rows] = dot3(source[start:, :], source[own_rows, :], 1, 1)
     share = bases[0].shape[0]
     index = sum(place[b] << b for b in range(bits - 1))
     leaf[...] = held[0][:, pl.ds(pl.multiple_of(index * share, share), share)]
@@ -143,14 +145,22 @@
         own, after = slice(start, start + PANEL), slice(start + PANEL, columns)
         last = start + PANEL == columns
         inverses = panel_inverses([gram[own, own] for gram in grams], hold)
-        for inverse, source, gram, basis in zip(inverses, held, grams, bases):
+        for m, (inverse, source, gram, basis) in enumerate(zip(inverses, held, grams, made)):
             if not last:
                 lower = dot3(gram[after, own], inverse, 1, 1)
-                gram[after, after] = gram[after, after] - dot3(lower, lower, 1, 1)
+                for at in range(start + PANEL, columns, PANEL):
+                    low = lower[at - start - PANEL :]
+                    cut = slice(at, at + PANEL)
+                    gram[at:, cut] = gram[at:, cut] - dot3(low, low[:PANEL], 1, 1)
             block = dot3(inverse, source[own, :], 1, 0)
             basis[:, own] = block.T * scale
+            target = bases[m].at[:, own]
+            copies.append(pltpu.make_async_copy(basis.at[:, own], target, sems.at[m, start // PANEL]))
+            copies[-1].start()
             if not last:
                 source[after, :] = source[after, :] - dot3(lower, block, 1, 0)
+    for copy in copies:
+        copy.wait()
 
 
 def bases_of(place, own, came, share):
@@ -162,10 +172,12 @@
         functools.partial(basis_kernel, count=count, bits=bits),
         out_shape=[jax.ShapeDtypeStruct(shape, F32) for shape in shapes],
         in_specs=[SMEM, VMEM, VMEM],
-        out_specs=[VMEM] * count,
+        out_specs=[pl.BlockSpec(memory_space=pltpu.HBM)] * count,
         scratch_shapes=[pltpu.VMEM((columns, rows), F32)] * count
         + [pltpu.VMEM((columns, columns), F32)] * count
-        + [pltpu.VMEM((columns, share), F32), pltpu.VMEM((count, 4, STRIP // 8 + 1, 8, PANEL), F32)],
+        + [pltpu.VMEM((columns, share), F32), pltpu.VMEM((count, 4, STRIP // 8 + 1, 8, PANEL), F32)]
+        + [pltpu.VMEM(shape, F32) for shape in shapes]
+        + [pltpu.SemaphoreType.DMA((count, columns // PANEL))],
         compiler_params=pltpu.CompilerParams(vmem_limit_bytes=BASES_VMEM),
         name="bases",
     )(place, own, came)
@@ -182,10 +194,13 @@
     )(*operands)
 
 
-def pick(value, indices):
-    count, width = value.shape
+def one_hot(indices, width):
     lanes = lax.broadcasted_iota(jnp.int32, (width, indices.shape[1]), 0)
-    chosen = (lanes == indices).astype(BF16)
+    return (lanes == indices).astype(BF16)
+
+
+def pick_by(value, chosen):
+    count = value.shape[0]
     high = value.astype(BF16)
     rest = value - high.astype(F32)
     middle = rest.astype(BF16)
@@ -194,6 +209,10 @@
     return found[:count] + (found[count : 2 * count] + found[2 * count :])
 
 
+def pick(value, indices):
+    return pick_by(value, one_hot(indices, value.shape[1]))
+
+
 def ordered(first, second, swapped):
     return jnp.concatenate(
         [jnp.where(swapped, second, first), jnp.where(swapped, first, second)], 1
@@ -211,19 +230,28 @@
 def product_kernel(place, matrix, sketch, pivots, *refs, bits):
     own, other = refs[:2]
     tops = refs[2 : 2 + (1 << bits)]
-    rows_held, sketch_held, turned, found, sent, sems = refs[2 + (1 << bits) :]
+    rows_held, sketch_held, turned, sent, chosen, sems = refs[2 + (1 << bits) :]
     leaf, half, columns = matrix.shape[0] // 2, own.shape[0], sketch.shape[1]
     rank = pivots.shape[2]
     sketch_copy = pltpu.make_async_copy(sketch, sketch_held, sems.at[2])
     sketch_copy.start()
+    pivots_copy = pltpu.make_async_copy(pivots, chosen, sems.at[3])
+    pivots_copy.start()
     copies = []
     for step in range(2):
         rows = pl.ds(step * leaf, leaf)
         copies.append(pltpu.make_async_copy(matrix.at[rows], rows_held.at[rows], sems.at[step]))
         copies[-1].start()
+    pivots_copy.wait()
+    last = one_hot(chosen[2], 2 * rank)
+    both = [
+        dot_of(one_hot(chosen[n], leaf), last[n * rank : n * rank + rank], 1, 0).astype(BF16)
+        for n in range(2)
+    ]
     sketch_copy.wait()
     turned[...] = sketch_held[...].T
     second = place[0] == 1
+    picked = None
     for step, copy in enumerate(copies):
         copy.wait()
         lanes = slice(step * leaf, step * leaf + leaf)
@@ -231,8 +259,9 @@
         near, far = value[:half], value[half:]
         own[:, lanes] = jnp.where(second, far, near)
         other[:, lanes] = jnp.where(second, near, far)
-        found[:, step * rank : step * rank + rank] = pick(value, pivots[step])
-    sent[...] = pick(found[...], pivots[2])
+        found = pick_by(value, both[step])
+        picked = found if picked is None else picked + found
+    sent[...] = picked
     for x, top in enumerate(tops):
         size = top.shape[0]
         start = chunk_start(place, bits, x, columns)
@@ -247,15 +276,15 @@
     return pl.pallas_call(
         functools.partial(product_kernel, bits=bits),
         out_shape=[jax.ShapeDtypeStruct(shape, F32) for shape in shapes],
-        in_specs=[SMEM, hbm, hbm, VMEM],
+        in_specs=[SMEM, hbm, hbm, hbm],
         out_specs=[VMEM] * len(shapes),
         scratch_shapes=[
             pltpu.VMEM(matrix.shape, BF16),
             pltpu.VMEM(sketch.shape, BF16),
             pltpu.VMEM((columns, depth), BF16),
-            pltpu.VMEM((columns, 2 * rank), F32),
             pltpu.VMEM((columns, rank), F32),
-            pltpu.SemaphoreType.DMA((3,)),
+            pltpu.VMEM(pivots.shape, jnp.int32),
+            pltpu.SemaphoreType.DMA((4,)),
         ],
         compiler_params=pltpu.CompilerParams(vmem_limit_bytes=PRODUCT_VMEM),
         name="product",
@@ -268,7 +297,8 @@
     other[...] = part(held, 1 - place[bit], half) + part(came, 1 - place[bit], half)
 
 
-def add_and_part(place, held, came, pivots, gate, own, kept, sent, *, bit):
+def add_and_part(place, held, came, pivots, *refs, bit):
+    own, kept, sent = refs[-3:]
     leaf = own.shape[1]
     parts = []
     for index in (place[bit], 1 - place[bit]):

time: 63.3 us -> 63 us (level)
  no operation moved by 1% of the time
where the time goes in v4:
time: 63 us; the launch traced here: 62.8 us
  Pallas kernels  29 us (46%)
  waiting for transfers between devices  17.7 us (28%)
  starting transfers between devices  14.5 us (23%)
  between operations  0.87 us (1%)
  local copies, waits for them, and re-layouts  0.69 us (1%)
    pallas_call x1, Pallas kernels, bases_of(): pl.pallas_call(functools.partial(basis_kernel, count=count, bits=bits), o...  18.5 us
    ppermute x6, waiting for transfers between devices, exchange(): lax.ppermute(block, 'samples', [(s, s ^ other) for s in range(count)])  7.98 us
    pallas_call x1, Pallas kernels, product(): pl.pallas_call(functools.partial(product_kernel, bits=bits), out_shape=[j...  6.67 us
    ppermute x3, waiting for transfers between devices, climb(): lax.ppermute(current, 'rows', [(d, d ^ step) for d in range(count)])  4.71 us
    ppermute x6, starting transfers between devices, exchange(): lax.ppermute(block, 'samples', [(s, s ^ other) for s in range(count)])  4.52 us
    pallas_call x4, Pallas kernels, call(): pl.pallas_call(functools.partial(kernel, **static), out_shape=[jax.ShapeD...  3.82 us
    ppermute x3, starting transfers between devices, climb(): lax.ppermute(current, 'rows', [(d, d ^ step) for d in range(count)])  3.49 us
    ppermute x1, starting transfers between devices, climb(): second = lax.ppermute(second, axes, other_side)  3.36 us
  transfers between devices with their start and end apart: 12, of which 7 were waited for; matrix products, arithmetic and copies ran while one was open for 0% of the time, Pallas kernels for 3%

profile of v4, /device:TPU:0, one launch (start us, length us, event | category | flops | bytes accessed | tf_op | source)
XLA Modules:
  0.0 62.8 jit_solution(7197874773453665182)
XLA Ops:
  0.6 0.1 pad_add_fusion.place.refs_0_
  0.7 0.0 copy-start
  0.7 0.7 %copy-done = s32[1,3,256]{2,0,1:T(1,128)S(1)} copy-done((s32[1,3,256]{2,0,1:T(1,128)S(1)}, s32[1,3,256]{2,0,1:T(1,128)}, u32[]{:S(2)}) %copy-start) | copy-done | bytes 3096
  1.4 6.7 %product.1 = (f32[192,1024]{1,0:T(8,128)S(1)}, f32[192,1024]{1,0:T(8,128)S(1)}, f32[96,256]{1,0:T(8,128)S(1)}, f32[96,256]{1,0:T(8,128)S(1)}, f32[96,256]{1,0:T(8,128)S(1)}, /*index=5*/f32[96,256]{1,0:T(8,128)S(1)}) custom-call(s32[3]{0:T(128)S(1)} %pad_add_fusion.place.refs_0_, bf16[1024,2560]{1,0:T(8,128)(2,1)} %matrix.1, bf16[2560,384]{1,0:T(8,128)(2,1)} %sketch.1, ...), custom_call_target="tpu_custom_call" | custom-call | tf_op jit(solution)/shard_map/product/pallas_call | solution.py:276
  8.1 0.0 copy-start.1
  8.1 0.5 collective-permute-start.9
  8.6 0.1 collective-permute-start
  8.7 2.9 %collective-permute-start.1 = (f32[96,256]{1,0:T(8,128)S(1)}, f32[96,256]{1,0:T(8,128)S(1)}, u32[]{:S(2)}, u32[]{:S(2)}) collective-permute-start(f32[96,256]{1,0:T(8,128)S(1)} %get-tuple-element.22), channel_id=1, source_target_pairs={{0,2},{1,3},{2,0},{3,1},{4,6},{5,7},{6,4},{7,5},{8,10},{9,11},{10,... | collective-permute-start | bytes 294920 | tf_op jit(solution)/shard_map/ppermute | solution.py:381
  11.6 0.0 collective-permute-start.2
  11.6 0.0 collective-permute-done.refs_1_
  11.6 3.2 %collective-permute-done.1.refs_2_ = f32[96,256]{1,0:T(8,128)S(1)} collective-permute-done((f32[96,256]{1,0:T(8,128)S(1)}, f32[96,256]{1,0:T(8,128)S(1)}, u32[]{:S(2)}, u32[]{:S(2)}) %collective-permute-start.1) | collective-permute-done | bytes 98336 | tf_op jit(solution)/shard_map/ppermute | solution.py:381
  14.8 2.0 %collective-permute-done.2.refs_3_ = f32[96,256]{1,0:T(8,128)S(1)} collective-permute-done((f32[96,256]{1,0:T(8,128)S(1)}, f32[96,256]{1,0:T(8,128)S(1)}, u32[]{:S(2)}, u32[]{:S(2)}) %collective-permute-start.2) | collective-permute-done | bytes 98336 | tf_op jit(solution)/shard_map/ppermute | solution.py:381
  16.7 0.6 add_all.1.own.refs_0_
  17.3 0.0 collective-permute-done.9.came
  17.3 1.1 %add_and_part.1 = (f32[192,512]{1,0:T(8,128)S(1)}, f32[192,256]{1,0:T(8,128)S(1)}, f32[192,768]{1,0:T(8,128)S(1)}) custom-call(s32[3]{0:T(128)S(1)} %pad_add_fusion.place.refs_0_, f32[192,1024]{1,0:T(8,128)S(1)} %get-tuple-element.28.held, f32[192,1024]{1,0:T(8,128)S(1)} %collective-permute-done.9.came, s32[3,1,256]{2,1,0:T(1,128)S(1)} %bitcast.5, ...), custom_call_target="tpu_custom_call" | custom-call | tf_op jit(solution)/shard_map/add_and_part/pallas_call | solution.py:187
  18.4 0.9 %collective-permute-start.10 = (f32[192,768]{1,0:T(8,128)S(1)}, f32[192,768]{1,0:T(8,128)S(1)}, u32[]{:S(2)}, u32[]{:S(2)}) collective-permute-start(f32[192,768]{1,0:T(8,128)S(1)} %get-tuple-element.30), channel_id=1, source_target_pairs={{0,2},{1,3},{2,0},{3,1},{4,6},{5,7},{6,4},{7,5},{8,10},{9,11},{10,... | collective-permute-start | bytes 1769480 | tf_op jit(solution)/shard_map/ppermute | solution.py:381
  19.4 2.5 %collective-permute-start.5 = (f32[96,256]{1,0:T(8,128)S(1)}, f32[96,256]{1,0:T(8,128)S(1)}, u32[]{:S(2)}, u32[]{:S(2)}) collective-permute-start(f32[96,256]{1,0:T(8,128)S(1)} %add_all.1.own.refs_0_), channel_id=1, source_target_pairs={{0,12},{4,8},{8,4},{12,0},{16,28},{20,24},{24,20},{28,16},{1,13},{... | collective-permute-start | bytes 294920 | tf_op jit(solution)/shard_map/ppermute | solution.py:393
  21.9 0.5 collective-permute-start.4
  22.3 0.5 collective-permute-start.3
  22.8 3.0 %collective-permute-done.5.next_3 = f32[96,256]{1,0:T(8,128)S(1)} collective-permute-done((f32[96,256]{1,0:T(8,128)S(1)}, f32[96,256]{1,0:T(8,128)S(1)}, u32[]{:S(2)}, u32[]{:S(2)}) %collective-permute-start.5) | collective-permute-done | bytes 98336 | tf_op jit(solution)/shard_map/ppermute | solution.py:393
  25.9 1.7 %collective-permute-done.4.next_2 = f32[96,256]{1,0:T(8,128)S(1)} collective-permute-done((f32[96,256]{1,0:T(8,128)S(1)}, f32[96,256]{1,0:T(8,128)S(1)}, u32[]{:S(2)}, u32[]{:S(2)}) %collective-permute-start.4) | collective-permute-done | bytes 98336 | tf_op jit(solution)/shard_map/ppermute | solution.py:393
  27.6 0.0 collective-permute-done.3.next_1
  27.6 0.0 copy-done.1
  27.6 1.2 %two_levels.1 = (f32[96,512]{1,0:T(8,128)S(1)}, f32[96,256]{1,0:T(8,128)S(1)}, f32[96,256]{1,0:T(8,128)S(1)}, f32[96,256]{1,0:T(8,128)S(1)}) custom-call(s32[3]{0:T(128)S(1)} %pad_add_fusion.place.refs_0_, f32[96,256]{1,0:T(8,128)S(1)} %add_all.1.own.refs_0_, f32[96,256]{1,0:T(8,128)S(1)} %collective-permute-done.3.next_1, ...), custom_call_target="tpu_custom_call" | custom-call | tf_op jit(solution)/shard_map/two_levels/pallas_call | solution.py:187
  28.8 0.7 %collective-permute-start.6 = (f32[96,256]{1,0:T(8,128)S(1)}, f32[96,256]{1,0:T(8,128)S(1)}, u32[]{:S(2)}, u32[]{:S(2)}) collective-permute-start(f32[96,256]{1,0:T(8,128)S(1)} %get-tuple-element.26), channel_id=1, source_target_pairs={{0,2},{1,3},{2,0},{3,1},{4,6},{5,7},{6,4},{7,5},{8,10},{9,11},{10,... | collective-permute-start | bytes 294920 | tf_op jit(solution)/shard_map/ppermute | solution.py:418
  29.5 3.4 %collective-permute-start.7 = (f32[96,256]{1,0:T(8,128)S(1)}, f32[96,256]{1,0:T(8,128)S(1)}, u32[]{:S(2)}, u32[]{:S(2)}) collective-permute-start(f32[96,256]{1,0:T(8,128)S(1)} %get-tuple-element.27), channel_id=1, source_target_pairs={{0,18},{1,19},{2,16},{3,17},{4,6},{5,7},{6,4},{7,5},{8,10},{9,11},... | collective-permute-start | bytes 294920 | tf_op jit(solution)/shard_map/ppermute | solution.py:419
  32.9 2.4 %collective-permute-start.8 = (f32[96,256]{1,0:T(8,128)S(1)}, f32[96,256]{1,0:T(8,128)S(1)}, u32[]{:S(2)}, u32[]{:S(2)}) collective-permute-start(f32[96,256]{1,0:T(8,128)S(1)} %get-tuple-element.25.top), channel_id=1, source_target_pairs={{0,16},{1,17},{2,18},{3,19},{16,0},{17,1},{18,2},{19,3}} | collective-permute-start | bytes 294920 | tf_op jit(solution)/shard_map/ppermute | solution.py:420
  35.3 2.7 %collective-permute-done.6.first = f32[96,256]{1,0:T(8,128)S(1)} collective-permute-done((f32[96,256]{1,0:T(8,128)S(1)}, f32[96,256]{1,0:T(8,128)S(1)}, u32[]{:S(2)}, u32[]{:S(2)}) %collective-permute-start.6) | collective-permute-done | bytes 98336 | tf_op jit(solution)/shard_map/ppermute | solution.py:418
  38.0 0.0 collective-permute-done.7.second
  38.0 2.3 %collective-permute-done.8.third = f32[96,256]{1,0:T(8,128)S(1)} collective-permute-done((f32[96,256]{1,0:T(8,128)S(1)}, f32[96,256]{1,0:T(8,128)S(1)}, u32[]{:S(2)}, u32[]{:S(2)}) %collective-permute-start.8) | collective-permute-done | bytes 98336 | tf_op jit(solution)/shard_map/ppermute | solution.py:420
  40.3 0.0 collective-permute-done.10.came
  40.3 0.9 %join_all.1.refs_1_ = f32[192,1536]{1,0:T(8,128)S(1)} custom-call(s32[3]{0:T(128)S(1)} %pad_add_fusion.place.refs_0_, f32[96,512]{1,0:T(8,128)S(1)} %get-tuple-element.24.node, f32[96,256]{1,0:T(8,128)S(1)} %get-tuple-element.25.top, f32[96,256]{1,0:T(8,128)S(1)} %collective-permute-done.6.first, f32[96,256]{1,0:T(8,128)S(1)} %collective-permute-done.7.second, ...), custom_call_target="tpu_custom_call" | custom-call | tf_op jit(solution)/shard_map/join_all/pallas_call | solution.py:187
  41.3 0.1 collective-permute-start.11
  41.3 2.8 %collective-permute-done.11.refs_2_ = f32[192,1536]{1,0:T(8,128)S(1)} collective-permute-done((f32[192,1536]{1,0:T(8,128)S(1)}, f32[192,1536]{1,0:T(8,128)S(1)}, u32[]{:S(2)}, u32[]{:S(2)}) %collective-permute-start.11) | collective-permute-done | bytes 1179680 | tf_op jit(solution)/shard_map/ppermute | solution.py:381
  44.2 18.5 %bases.1 = (f32[256,384]{1,0:T(8,128)}, f32[512,384]{1,0:T(8,128)}, f32[512,384]{1,0:T(8,128)}) custom-call(s32[3]{0:T(128)S(1)} %pad_add_fusion.place.refs_0_, f32[192,1536]{1,0:T(8,128)S(1)} %join_all.1.refs_1_, f32[192,1536]{1,0:T(8,128)S(1)} %collective-permute-done.11.refs_2_), custom_call_target="tpu_custom_call" | custom-call | tf_op jit(solution)/shard_map/bases/pallas_call | solution.py:171
Async XLA Ops:
  0.7 0.7 %copy-start = (s32[1,3,256]{2,0,1:T(1,128)S(1)}, s32[1,3,256]{2,0,1:T(1,128)}, u32[]{:S(2)}) copy-start(s32[1,3,256]{2,0,1:T(1,128)} %param.6) | copy-start | bytes 9220
  8.1 19.5 %copy-start.1 = (s32[6,256]{1,0:T(8,128)S(1)}, s32[6,256]{1,0:T(8,128)}, u32[]{:S(2)}) copy-start(s32[6,256]{1,0:T(8,128)} %upper.1) | copy-start | bytes 18436
  8.1 9.2 %collective-permute-start.9 = (f32[192,1024]{1,0:T(8,128)S(1)}, f32[192,1024]{1,0:T(8,128)S(1)}, u32[]{:S(2)}, u32[]{:S(2)}) collective-permute-start(f32[192,1024]{1,0:T(8,128)S(1)} %get-tuple-element.29), channel_id=1, source_target_pairs={{0,1},{1,0},{2,3},{3,2},{4,5},{5,4},{6,7},{7,6},{8,9},{9,8},{10,11... | collective-permute-start | bytes 2359304 | tf_op jit(solution)/shard_map/ppermute | solution.py:381
  8.6 3.0 %collective-permute-start = (f32[96,256]{1,0:T(8,128)S(1)}, f32[96,256]{1,0:T(8,128)S(1)}, u32[]{:S(2)}, u32[]{:S(2)}) collective-permute-start(f32[96,256]{1,0:T(8,128)S(1)} %get-tuple-element.21), channel_id=1, source_target_pairs={{0,1},{1,0},{2,3},{3,2},{4,5},{5,4},{6,7},{7,6},{8,9},{9,8},{10,11... | collective-permute-start | bytes 294920 | tf_op jit(solution)/shard_map/ppermute | solution.py:381
  8.7 6.1 %collective-permute-start.1 = (f32[96,256]{1,0:T(8,128)S(1)}, f32[96,256]{1,0:T(8,128)S(1)}, u32[]{:S(2)}, u32[]{:S(2)}) collective-permute-start(f32[96,256]{1,0:T(8,128)S(1)} %get-tuple-element.22), channel_id=1, source_target_pairs={{0,2},{1,3},{2,0},{3,1},{4,6},{5,7},{6,4},{7,5},{8,10},{9,11},{10,... | collective-permute-start | bytes 294920 | tf_op jit(solution)/shard_map/ppermute | solution.py:381
  11.6 5.1 %collective-permute-start.2 = (f32[96,256]{1,0:T(8,128)S(1)}, f32[96,256]{1,0:T(8,128)S(1)}, u32[]{:S(2)}, u32[]{:S(2)}) collective-permute-start(f32[96,256]{1,0:T(8,128)S(1)} %get-tuple-element.23), channel_id=1, source_target_pairs={{0,3},{1,2},{2,1},{3,0},{4,7},{5,6},{6,5},{7,4},{8,11},{9,10},{10,... | collective-permute-start | bytes 294920 | tf_op jit(solution)/shard_map/ppermute | solution.py:381
  18.4 21.9 %collective-permute-start.10 = (f32[192,768]{1,0:T(8,128)S(1)}, f32[192,768]{1,0:T(8,128)S(1)}, u32[]{:S(2)}, u32[]{:S(2)}) collective-permute-start(f32[192,768]{1,0:T(8,128)S(1)} %get-tuple-element.30), channel_id=1, source_target_pairs={{0,2},{1,3},{2,0},{3,1},{4,6},{5,7},{6,4},{7,5},{8,10},{9,11},{10,... | collective-permute-start | bytes 1769480 | tf_op jit(solution)/shard_map/ppermute | solution.py:381
  19.4 6.5 %collective-permute-start.5 = (f32[96,256]{1,0:T(8,128)S(1)}, f32[96,256]{1,0:T(8,128)S(1)}, u32[]{:S(2)}, u32[]{:S(2)}) collective-permute-start(f32[96,256]{1,0:T(8,128)S(1)} %add_all.1.own.refs_0_), channel_id=1, source_target_pairs={{0,12},{4,8},{8,4},{12,0},{16,28},{20,24},{24,20},{28,16},{1,13},{... | collective-permute-start | bytes 294920 | tf_op jit(solution)/shard_map/ppermute | solution.py:393
  21.9 5.7 %collective-permute-start.4 = (f32[96,256]{1,0:T(8,128)S(1)}, f32[96,256]{1,0:T(8,128)S(1)}, u32[]{:S(2)}, u32[]{:S(2)}) collective-permute-start(f32[96,256]{1,0:T(8,128)S(1)} %add_all.1.own.refs_0_), channel_id=1, source_target_pairs={{0,8},{4,12},{8,0},{12,4},{16,24},{20,28},{24,16},{28,20},{1,9},{5... | collective-permute-start | bytes 294920 | tf_op jit(solution)/shard_map/ppermute | solution.py:393
  22.3 5.2 %collective-permute-start.3 = (f32[96,256]{1,0:T(8,128)S(1)}, f32[96,256]{1,0:T(8,128)S(1)}, u32[]{:S(2)}, u32[]{:S(2)}) collective-permute-start(f32[96,256]{1,0:T(8,128)S(1)} %add_all.1.own.refs_0_), channel_id=1, source_target_pairs={{0,4},{4,0},{8,12},{12,8},{16,20},{20,16},{24,28},{28,24},{1,5},{5... | collective-permute-start | bytes 294920 | tf_op jit(solution)/shard_map/ppermute | solution.py:393
  28.8 9.3 %collective-permute-start.6 = (f32[96,256]{1,0:T(8,128)S(1)}, f32[96,256]{1,0:T(8,128)S(1)}, u32[]{:S(2)}, u32[]{:S(2)}) collective-permute-start(f32[96,256]{1,0:T(8,128)S(1)} %get-tuple-element.26), channel_id=1, source_target_pairs={{0,2},{1,3},{2,0},{3,1},{4,6},{5,7},{6,4},{7,5},{8,10},{9,11},{10,... | collective-permute-start | bytes 294920 | tf_op jit(solution)/shard_map/ppermute | solution.py:418
  29.5 8.5 %collective-permute-start.7 = (f32[96,256]{1,0:T(8,128)S(1)}, f32[96,256]{1,0:T(8,128)S(1)}, u32[]{:S(2)}, u32[]{:S(2)}) collective-permute-start(f32[96,256]{1,0:T(8,128)S(1)} %get-tuple-element.27), channel_id=1, source_target_pairs={{0,18},{1,19},{2,16},{3,17},{4,6},{5,7},{6,4},{7,5},{8,10},{9,11},... | collective-permute-start | bytes 294920 | tf_op jit(solution)/shard_map/ppermute | solution.py:419
  32.9 7.4 %collective-permute-start.8 = (f32[96,256]{1,0:T(8,128)S(1)}, f32[96,256]{1,0:T(8,128)S(1)}, u32[]{:S(2)}, u32[]{:S(2)}) collective-permute-start(f32[96,256]{1,0:T(8,128)S(1)} %get-tuple-element.25.top), channel_id=1, source_target_pairs={{0,16},{1,17},{2,18},{3,19},{16,0},{17,1},{18,2},{19,3}} | collective-permute-start | bytes 294920 | tf_op jit(solution)/shard_map/ppermute | solution.py:420
  41.3 2.9 %collective-permute-start.11 = (f32[192,1536]{1,0:T(8,128)S(1)}, f32[192,1536]{1,0:T(8,128)S(1)}, u32[]{:S(2)}, u32[]{:S(2)}) collective-permute-start(f32[192,1536]{1,0:T(8,128)S(1)} %join_all.1.refs_1_), channel_id=1, source_target_pairs={{0,1},{1,0},{2,3},{3,2},{4,5},{5,4},{6,7},{7,6},{8,9},{9,8},{10,11... | collective-permute-start | bytes 3538952 | tf_op jit(solution)/shard_map/ppermute | solution.py:381
